TPU v7x, 32 devices: a whole 2x2x4 slice. The times are simulated.
32 devices in a mesh: ctx: 16 (over z, y, core), tp: 2 (over x).
Axes of the slice: x: 2, y: 2, z: 4, core: 2. Of those that a mesh axis runs over, the one named last changes fastest.
Arguments:
- inputs: float32 [4096, 5120], P('ctx', 'tp'), may hold values from -6 to 6
- state_input: float32 [4096, 128], P('ctx'), may hold values from -0.125 to 0.125
- state_output: float32 [4096, 128], P('ctx'), may hold values from -0.125 to 0.125
- decay_codes: int32 [80, 4096], P('tp', 'ctx'), may hold values from 0 to 45000
- output_grad: float32 [4096, 5120], P('ctx', 'tp'), may hold values from -6 to 6
Outputs:
- input_grad: float32 [4096, 5120], P('ctx', 'tp')
- b_grad: float32 [4096, 128], P(('ctx', 'tp'))
- c_grad: float32 [4096, 128], P(('ctx', 'tp'))
- decay_grad: float32 [80, 4096], P('tp', 'ctx')
All inputs are finite; a program needn't handle non-finite values.
Results may differ from a plain program's by a relative error of at most 0.00029.
Values sent between devices are 32-bit elements; how exact they have to be, the bound alone decides.
A program may use at most 128 MiB of HBM per device.

v0:
```python
import jax
import jax.numpy as jnp
from jax import lax
from jax.sharding import PartitionSpec as P

Q = 256


PRECISE = lax.Precision.HIGHEST
CODE_UNIT = 2.0 ** (-16)


def carried_in(part, axis, combine, identity, reverse):
    count = lax.axis_size(axis)
    place = lax.axis_index(axis)
    ahead = count - 1 - place if reverse else place
    gathered = jax.tree.map(lambda a: lax.all_gather(a, axis), part)
    state = jax.tree.map(lambda a, e: jnp.zeros_like(a) + jnp.asarray(e, a.dtype), part, identity)

    def one(step, state):
        source = count - 1 - step if reverse else step
        return combine(
            state, jax.tree.map(lambda a: lax.dynamic_index_in_dim(a, source, 0, False), gathered)
        )

    return lax.fori_loop(0, ahead, one, state)


def decay_parts(log_decay):
    within = jnp.cumsum(log_decay, axis=-1)
    return (within, within[..., -1])


def block_states(values, writers, within, final_log):
    tail_decay = jnp.exp(final_log[..., None] - within)
    return jnp.einsum("hks,hksp,ksn->hkpn", tail_decay, values, writers, precision=PRECISE)


def fold_blocks(start_state, factors, pieces):

    def carry_step(carried_state, element):
        factor, portion = element
        return (factor[:, None, None] * carried_state + portion, carried_state)

    return lax.scan(
        carry_step, start_state, (jnp.moveaxis(factors, 1, 0), jnp.moveaxis(pieces, 1, 0))
    )


def ssd_forward(values, writers, readers, log_decay, start_state):
    within, final_log = decay_parts(log_decay)
    row_index = lax.broadcasted_iota(jnp.int32, (Q, Q), 0)
    column_index = lax.broadcasted_iota(jnp.int32, (Q, Q), 1)
    causal = column_index <= row_index
    log_gap = within[..., :, None] - within[..., None, :]
    decay_matrix = jnp.where(causal, jnp.exp(jnp.where(causal, log_gap, 0.0)), 0.0)
    scores = jnp.einsum("ktn,ksn->kts", readers, writers, precision=PRECISE)
    intra_out = jnp.einsum(
        "hkts,hksp->hktp", decay_matrix * scores[None], values, precision=PRECISE
    )
    pieces = block_states(values, writers, within, final_log)
    end_state, entering = fold_blocks(start_state, jnp.exp(final_log), pieces)
    entering = jnp.moveaxis(entering, 0, 1)
    inter_out = jnp.exp(within)[..., None] * jnp.einsum(
        "ktn,hkpn->hktp", readers, entering, precision=PRECISE
    )
    return (intra_out + inter_out, end_state)


def split_heads(flat, head_count):
    row_count = flat.shape[0]
    return jnp.transpose(flat.reshape(row_count, head_count, -1), (1, 0, 2)).reshape(
        head_count, row_count // Q, Q, -1
    )


def combine_states(earlier, later):
    return (earlier[0] * later[0], later[0][:, None, None] * earlier[1] + later[1])


def per_device(inputs, state_input, state_output, decay_codes, output_grad):
    head_count = decay_codes.shape[0]
    row_count = inputs.shape[0]
    block_count = row_count // Q
    head_inputs = split_heads(inputs, head_count)
    head_grads = split_heads(output_grad, head_count)
    head_width = head_inputs.shape[-1]
    state_width = state_input.shape[1]
    writers = state_input.reshape(block_count, Q, state_width)
    readers = state_output.reshape(block_count, Q, state_width)
    log_decay = (-decay_codes.astype(jnp.float32) * CODE_UNIT).reshape(head_count, block_count, Q)
    within, final_log = decay_parts(log_decay)
    empty_state = jnp.zeros((head_count, head_width, state_width), jnp.float32)
    pieces = block_states(head_inputs, writers, within, final_log)
    local_end, _ = fold_blocks(empty_state, jnp.exp(final_log), pieces)
    device_decay = jnp.exp(jnp.sum(final_log, axis=1))
    unit_decay = jnp.ones((head_count,), jnp.float32)
    start_state = carried_in(
        (device_decay, local_end), "ctx", combine_states, (unit_decay, empty_state), False
    )[1]
    before = jnp.exp(jnp.cumsum(final_log, axis=1) - final_log)
    weights = jnp.exp(within) * before[..., None]
    pulled = jnp.einsum("hkt,hktp,ktn->hpn", weights, head_grads, readers, precision=PRECISE)
    end_cotangent = carried_in(
        (device_decay, pulled), "ctx", combine_states, (unit_decay, empty_state), True
    )[1]

    def whole(values, writers_in, readers_in, decay_in, state_in):
        return ssd_forward(values, writers_in, readers_in, decay_in, state_in)

    _, pullback = jax.vjp(whole, head_inputs, writers, readers, log_decay, start_state)
    grads = pullback((head_grads, end_cotangent))[:4]
    value_grad, writer_grad, reader_grad, decay_grad = grads
    input_grad = jnp.transpose(
        value_grad.reshape(head_count, row_count, head_width), (1, 0, 2)
    ).reshape(row_count, head_count * head_width)
    row_sums = (
        lax.psum_scatter(
            writer_grad.reshape(row_count, state_width), "tp", scatter_dimension=0, tiled=True
        ),
        lax.psum_scatter(
            reader_grad.reshape(row_count, state_width), "tp", scatter_dimension=0, tiled=True
        ),
    )
    return (input_grad, row_sums[0], row_sums[1], decay_grad.reshape(head_count, row_count))


def solution(mesh):
    placed = (P("ctx", "tp"), P("ctx", None), P("ctx", None), P("tp", "ctx"), P("ctx", "tp"))
    return jax.shard_map(
        per_device,
        mesh=mesh,
        in_specs=placed,
        out_specs=(P("ctx", "tp"), P(("ctx", "tp"), None), P(("ctx", "tp"), None), P("tp", "ctx")),
        check_vma=False,
    )
```

profile of v0, /device:TPU:0, one launch (start us, length us, event | category | flops | bytes accessed | tf_op | source)
XLA Modules:
  0.0 339.6 jit_solution(2333182350522829264)
XLA Ops:
  7.2 0.8 negate_multiply_fusion
  8.1 0.6 reduce-window.14
  8.7 0.2 slice_reduce_fusion.1
  9.0 0.1 copy.52
  9.0 2.2 copy.54
  11.2 0.1 broadcast.78
  11.4 1.7 multiply_reduce_fusion.2
  13.1 0.6 fusion.50
  13.7 0.1 broadcast_multiply_fusion
  13.8 3.3 fusion.17
  17.1 0.0 reduce-scatter.3.cloned.1.call-start
  17.2 2.2 copy.55
  19.4 0.7 dynamic-slice.2
  20.7 0.2 dynamic-update-slice
  21.0 35.9 %all-reduce.1 = f32[640]{0:T(1024)S(1)} all-reduce(f32[640]{0:T(1024)S(1)} %dynamic-update-slice), channel_id=2, replica_groups=mesh['ctx'=16,'tp'=2] {'ctx'}, use_global_device_ids=true, to_apply=%add.1 | all-reduce | flops 640 | bytes 5120
  56.9 0.1 reshape.372
  57.1 0.4 fusion.51
  57.4 16.9 %fusion.5 = (f32[40,256]{1,0:T(8,128)}, f32[40,256]{1,0:T(8,128)}, f32[256,256]{1,0:T(8,128)S(1)}) fusion(f32[256,256]{1,0:T(8,128)S(1)} %fusion.51, f32[40,256]{1,0:T(8,128)S(1)} %get-tuple-element.231, pred[256,256]{1,0:T(8,128)(4,1)S(1)} %iota_compare_fusion, f32[40,256,64]{1,2,0:T(8,128)} %bitcast.148, f32[40,256,64]{1,2,0:T(8,128)S(1)} %bitcast.143), kind=kOutput, calls=%fused_computation.11 | convolution fusion | flops 2042015744 | bytes 5955584 | tf_op jit(solution)/shard_map/transpose(jvp(hkts,hksp->hktp))/dot_general | solution.py:58
  74.4 0.4 convolution_bitcast_fusion
  74.8 54.4 %all-gather.6.cloned.1.call-done = f32[640,64,128]{2,1,0:T(8,128)} async-done(((f32[40,64,128]{2,1,0:T(8,128)}), f32[640,64,128]{2,1,0:T(8,128)}) %all-gather.6.cloned.1.call-update) | async-done | bytes 20971536 | tf_op jit(solution)/shard_map/all_gather | solution.py:17
  129.2 0.1 broadcast_in_dim.57.clone
  129.3 24.6 %while.16 = (s32[]{:T(128)}, f32[40,64,128]{2,1,0:T(8,128)S(1)}, s32[]{:T(128)}, f32[16,40]{1,0:T(8,128)S(1)}, f32[16,40,64,128]{3,2,1,0:T(8,128)}, /*index=5*/s32[]{:T(128)}, s32[]{:T(128)}, s32[]{:T(128)}, s32[]{:T(128)}) while((s32[]{:T(128)}, f32[40,64,128]{2,1,0:T(8,128)S(1)}, s32[]{:T(128)}, f32[16,40]{1,0:T(8,128)S(1)}, ...), condition=%wide.region_3.4_spmd, body=%wide.region_2.3_spmd.sunk | while | flops 655366 | bytes 3932795 | solution.py:26
  129.4 1.6 bitcast_add_fusion.8
  131.0 1.6 bitcast_add_fusion.8
  132.6 1.6 bitcast_add_fusion.8
  134.2 1.6 bitcast_add_fusion.8
  135.8 1.6 bitcast_add_fusion.8
  137.5 1.6 bitcast_add_fusion.8
  139.1 1.6 bitcast_add_fusion.8
  140.7 1.6 bitcast_add_fusion.8
  142.3 1.6 bitcast_add_fusion.8
  144.0 1.6 bitcast_add_fusion.8
  145.6 1.6 bitcast_add_fusion.8
  147.2 1.6 bitcast_add_fusion.8
  148.8 1.6 bitcast_add_fusion.8
  150.5 1.6 bitcast_add_fusion.8
  152.1 1.6 bitcast_add_fusion.8
  153.9 5.6 %fusion.15 = (f32[40,256]{1,0:T(8,128)S(1)}, f32[40,64,256]{2,1,0:T(8,128)}) fusion(f32[40,256,64]{1,2,0:T(8,128)} %bitcast.144, f32[40,64,128]{2,1,0:T(8,128)S(1)} %get-tuple-element.183, f32[256,128]{1,0:T(8,128)S(1)} %copy-done), kind=kOutput, calls=%fused_computation.25 | convolution fusion | flops 1007933440 | bytes 6725632 | tf_op jit(solution)/shard_map/transpose(jvp(hks,hksp,ksn->hkpn))/dot_general | solution.py:36
  159.6 0.2 multiply_reduce_fusion.3
  159.8 3.0 fusion.38
  162.8 0.0 all-gather.8.cloned.1.call-start
  162.9 5.1 %fusion.25 = f32[40,64,128]{2,1,0:T(8,128)} fusion(f32[40,256,64]{1,2,0:T(8,128)} %bitcast.145, f32[40,256]{1,0:T(8,128)S(1)} %get-tuple-element.229, f32[40]{0:T(128)S(1)} %get-tuple-element.204, f32[256,128]{1,0:T(8,128)S(1)} %copy-done), kind=kOutput, calls=%fused_computation.33 | convolution fusion | flops 1007616000 | bytes 4104352 | tf_op jit(solution)/shard_map/hks,hksp,ksn->hkpn/dot_general | solution.py:36
  168.0 0.0 reduce-scatter.5.cloned.1.call-start
  168.1 12.2 %bitcast_add_fusion.2 = f32[40,1,256,64]{2,3,0,1:T(8,128)} fusion(f32[40,64,256]{2,1,0:T(8,128)} %get-tuple-element.234, f32[40,256,64]{1,2,0:T(8,128)} %bitcast.149, f32[256,256]{1,0:T(8,128)S(1)} %fusion.51, f32[40,256]{1,0:T(8,128)S(1)} %get-tuple-element.231, pred[256,256]{1,0:T(8,128)(4,1)S(1)} %copy-done.8, f32[40,256]{1,0:T(8,128)S(1)} %get-tuple-element.229), kind=kOutput, calls=%fused_computation.21 | convolution fusion | flops 2025062400 | bytes 8273920 | tf_op jit(solution)/shard_map/transpose(jvp(hkts,hksp->hktp))/dot_general | solution.py:58
  180.3 3.2 copy.62
  183.5 0.1 copy.58
  183.6 1.6 copy.63
  185.1 95.8 %all-gather.8.cloned.1.call-done = f32[640,64,128]{2,1,0:T(8,128)} async-done(((f32[40,64,128]{2,1,0:T(8,128)}), f32[640,64,128]{2,1,0:T(8,128)}) %all-gather.8.cloned.1.call-update) | async-done | bytes 20971536 | tf_op jit(solution)/shard_map/all_gather | solution.py:17
  281.0 0.1 broadcast_in_dim.57
  281.1 0.3 while.17
  281.4 0.4 multiply_reduce_fusion.1
  281.8 0.1 copy-done.6
  281.9 1.3 copy-done.4
  283.1 4.3 %fusion.41 = f32[256,128]{1,0:T(8,128)S(1)} fusion(f32[40,64,128]{2,1,0:T(8,128)S(1)} %get-tuple-element.184, f32[40,256,64]{1,2,0:T(8,128)S(1)} %bitcast.151, f32[40,256]{1,0:T(8,128)S(1)} %copy-done.6), kind=kOutput, calls=%fused_computation.44 | convolution fusion | flops 1007288320 | bytes 4104192 | tf_op jit(solution)/shard_map/transpose(jvp(ktn,hkpn->hktp))/dot_general | solution.py:64
  287.4 1.0 convolution_add_fusion
  288.5 0.1 copy.57
  288.6 4.0 %fusion.11 = f32[40,256]{1,0:T(8,128)S(1)} fusion(f32[40,1,256,64]{2,3,0,1:T(8,128)} %bitcast.150, f32[40,64,128]{2,1,0:T(8,128)S(1)} %get-tuple-element.184, f32[256,128]{1,0:T(8,128)S(1)} %copy-done.5), kind=kOutput, calls=%fused_computation.18 | convolution fusion | flops 1007933440 | bytes 4104192 | tf_op jit(solution)/shard_map/jvp(ktn,hkpn->hktp)/dot_general | solution.py:64
  292.6 0.1 pad_add_fusion
  292.7 2.5 reduce-window.16
  295.2 0.1 slice_reduce_fusion
  295.4 0.1 copy.61
  295.5 0.1 broadcast.79
  295.6 0.6 bitcast_add_fusion.3
  296.2 36.8 %reduce-scatter.5.cloned.1.call-done = f32[128,128]{1,0:T(8,128)} async-done(((f32[256,128]{1,0:T(8,128)}), f32[128,128]{1,0:T(8,128)}) %reduce-scatter.5.cloned.1.call-update) | async-done | bytes 65552 | tf_op jit(solution)/shard_map/reduce_scatter | solution.py:121
  (61 shorter events, 0.6 us)
Async XLA Ops:
  7.2 49.9 %copy-start = (f32[256,128]{1,0:T(8,128)S(1)}, f32[256,128]{1,0:T(8,128)}, u32[]{:S(2)}) copy-start(f32[256,128]{1,0:T(8,128)} %param.10) | copy-start | bytes 393220
  7.2 122.0 %all-gather.6.cloned.1.call-start = ((), (), s32[]{:S(2)}) async-start(), calls=%async_computation.4 | async-start | bytes 22282240 | tf_op jit(solution)/shard_map/all_gather | solution.py:17
  9.0 4.7 %copy-start.5 = (f32[256,128]{1,0:T(8,128)S(1)}, f32[256,128]{1,0:T(8,128)}, u32[]{:S(2)}) copy-start(f32[256,128]{1,0:T(8,128)} %param.11) | copy-start | bytes 393220
  11.2 5.8 %copy-start.3 = (f32[256,2560]{0,1:T(8,128)}, f32[256,2560]{0,1:T(8,128)S(1)}, u32[]{:S(2)}) copy-start(f32[256,2560]{0,1:T(8,128)S(1)} %copy.54) | copy-start | bytes 7864324
  17.1 166.5 %reduce-scatter.3.cloned.1.call-start = ((), (), s32[]{:S(2)}) async-start(), calls=%async_computation.2 | async-start | bytes 196608 | tf_op jit(solution)/shard_map/reduce_scatter | solution.py:118
  17.2 2.2 copy-start.13
  19.3 55.1 %copy-start.1 = (f32[256,2560]{0,1:T(8,128)}, f32[256,2560]{0,1:T(8,128)S(1)}, u32[]{:S(2)}) copy-start(f32[256,2560]{0,1:T(8,128)S(1)} %copy.55) | copy-start | bytes 7864324
  57.0 17.3 %copy-start.7 = (pred[256,256]{1,0:T(8,128)(4,1)}, pred[256,256]{1,0:T(8,128)(4,1)S(1)}, u32[]{:S(2)}) copy-start(pred[256,256]{1,0:T(8,128)(4,1)S(1)} %iota_compare_fusion) | copy-start | bytes 196612
  153.9 5.7 %copy-start.11 = (f32[16,40]{1,0:T(8,128)}, f32[16,40]{1,0:T(8,128)S(1)}, u32[]{:S(2)}) copy-start(f32[16,40]{1,0:T(8,128)S(1)} %get-tuple-element.365) | copy-start | bytes 7684
  153.9 5.7 %copy-start.12 = (f32[40]{0:T(128)S(1)}, f32[40]{0:T(128)}, u32[]{:S(2)}) copy-start(f32[40]{0:T(128)} %get-tuple-element.207) | copy-start | bytes 484
  153.9 5.9 %copy-start.2 = (f32[256,2560]{0,1:T(8,128)S(1)}, f32[256,2560]{0,1:T(8,128)}, u32[]{:S(2)}) copy-start(f32[256,2560]{0,1:T(8,128)} %copy-done.1) | copy-start | bytes 7864324
  162.8 118.1 %all-gather.8.cloned.1.call-start = ((), (), s32[]{:S(2)}) async-start(), calls=%async_computation.5 | async-start | bytes 22282240 | tf_op jit(solution)/shard_map/all_gather | solution.py:17
  162.9 5.2 %copy-start.8 = (pred[256,256]{1,0:T(8,128)(4,1)S(1)}, pred[256,256]{1,0:T(8,128)(4,1)}, u32[]{:S(2)}) copy-start(pred[256,256]{1,0:T(8,128)(4,1)} %copy-done.7) | copy-start | bytes 196612
  168.0 165.0 %reduce-scatter.5.cloned.1.call-start = ((), (), s32[]{:S(2)}) async-start(), calls=%async_computation.3 | async-start | bytes 196608 | tf_op jit(solution)/shard_map/reduce_scatter | solution.py:121
  281.1 0.8 copy-start.6
  281.4 1.7 copy-start.4
  287.4 5.1 %copy-start.9 = (f32[40,256]{1,0:T(8,128)S(1)}, f32[40,256]{1,0:T(8,128)}, u32[]{:S(2)}) copy-start(f32[40,256]{1,0:T(8,128)} %get-tuple-element.201) | copy-start | bytes 122884
  287.4 5.1 %copy-start.10 = (f32[40,256]{1,0:T(8,128)S(1)}, f32[40,256]{1,0:T(8,128)}, u32[]{:S(2)}) copy-start(f32[40,256]{1,0:T(8,128)} %get-tuple-element.202) | copy-start | bytes 122884
Sparse Core Ops, SparseCore 0:
  17.2 111.9 all-gather.5
  163.0 7.4 reduce-scatter.2
  172.1 108.8 all-gather.7
  288.6 44.4 reduce-scatter.4
where the time goes:
time: 341 us; the launch traced here: 340 us
  waiting for transfers between devices  187 us (55%)
  matrix products  56.2 us (16%)
  blocking collectives  35.9 us (11%)
  other arithmetic  31.5 us (9%)
  between operations  14.8 us (4%)
  local copies, waits for them, and re-layouts  12.9 us (4%)
    all_gather x2, waiting for transfers between devices, carried_in(): gathered = jax.tree.map(lambda a: lax.all_gather(a, axis), part)  150 us
    reduce_scatter x1, waiting for transfers between devices, per_device(): lax.psum_scatter(reader_grad.reshape(row_count, state_width), 'tp', scatt...  36.8 us
    unnamed x1, blocking collectives  35.9 us
    dot_general x2, matrix products, ssd_forward(): jnp.einsum('hkts,hksp->hktp', decay_matrix * scores[None], values, precis...  29.1 us
    add x15, other arithmetic, combine_states(): later[0][:, None, None] * earlier[1] + later[1]  23.7 us
    dot_general x3, matrix products, block_states(): jnp.einsum('hks,hksp,ksn->hkpn', tail_decay, values, writers, precision=P...  13.8 us
    unnamed x35, local copies, waits for them, and re-layouts  11.5 us
    dot_general x2, matrix products, ssd_forward(): jnp.einsum('ktn,hkpn->hktp', readers, entering, precision=PRECISE)  8.22 us
  transfers between devices with their start and end apart: 4, of which 3 were waited for; matrix products, arithmetic and copies ran while one was open for 15% of the time, Pallas kernels for 0%

commit v1 on v0

v1 whole, which is shorter than its diff:
```python
import functools

import jax
import jax.numpy as jnp
from jax import lax
from jax.experimental import pallas as pl
from jax.experimental.pallas import tpu as pltpu
from jax.sharding import PartitionSpec as P

MESH = pl.DeviceIdType.MESH
CODE_UNIT = 2.0 ** (-16)
LANES = 128
HALF = 64
F32 = jnp.float32
BF16 = jnp.bfloat16
NN = (((1,), (0,)), ((), ()))
NT = (((1,), (1,)), ((), ()))
TN = (((0,), (0,)), ((), ()))


def dot(a, b, dims=NN):
    return lax.dot_general(a, b, dims, preferred_element_type=F32)


def parts(a):
    high = a.astype(BF16)
    return high, (a - high.astype(F32)).astype(BF16)


def exact_dot(a, ones, dims):
    first = a.astype(BF16)
    rest = a - first.astype(F32)
    second = rest.astype(BF16)
    third = (rest - second.astype(F32)).astype(BF16)
    return dot(first, ones, dims) + dot(second, ones, dims) + dot(third, ones, dims)


def swap(a):
    return pltpu.roll(a, HALF, 1)


def kernel(
    ctx, tp, x_ref, b_ref, c_ref, code_ref, g_ref,
    dx_ref, db_ref, dc_ref, da_ref,
    wl, loc, dec, rdec0, dec1, rdec1, rbuf0, agg, rbuf1, zin, zout, zp, snd1, snd0, ent,
    score, dscore, rows_acc, col_acc, colq_acc, bc, rtp,
    cwide, bwide, send, recv,
):
    heads, toks = code_ref.shape
    pairs = x_ref.shape[1] // LANES
    two = pairs % 2 == 0
    four = pairs % 4 == 0
    hp = pairs // 2 if two else pairs
    qp = pairs // 4 if four else hp
    group = 4 if four else 2 if two else 1
    groups = ctx // group
    mid = toks // 2

    me = lax.axis_index("ctx")
    my_tp = lax.axis_index("tp")
    place = me // group
    core = me % 2 if two else 0
    side = (me // 2) % 2 if four else 0
    core_mate = me + 1 - 2 * (me % 2)
    side_mate = me + 2 - 4 * ((me // 2) % 2)
    half0 = core * hp if two else 0
    mine0 = side * qp if four else 0

    n_dec1 = 3
    n_up = 4
    n_chain = n_up + 2 * qp
    n_down = n_chain + 2 * qp
    n_last = n_down + 2 * qp
    n_tp = n_last + 2 * hp

    def copy(src, dst, number, to):
        return pltpu.make_async_remote_copy(
            src_ref=src, dst_ref=dst, send_sem=send.at[number], recv_sem=recv.at[number],
            device_id=to, device_id_type=MESH,
        )

    def up0(d):
        there = (1 - core) * hp
        return copy(loc.at[d, pl.ds(there, hp)], rbuf0.at[d], d, {"ctx": core_mate})

    def dec0_copy():
        return copy(dec, rdec0, 2, {"ctx": core_mate})

    def dec1_copy():
        return copy(dec1, rdec1, n_dec1, {"ctx": side_mate})

    def up1(d, k):
        return copy(
            agg.at[d, (1 - side) * qp + k], rbuf1.at[d, k], n_up + d * qp + k, {"ctx": side_mate}
        )

    def chain(d, k):
        to = me + group if d == 0 else me - group
        return copy(zout.at[d, k], zin.at[d, k], n_chain + d * qp + k, {"ctx": to})

    def down1(d, k):
        return copy(
            snd1.at[d, k], zp.at[d, mine0 + k], n_down + d * qp + k, {"ctx": side_mate}
        )

    def down0(d, k):
        return copy(
            snd0.at[d, k], ent.at[d, half0 + k], n_last + d * hp + k, {"ctx": core_mate}
        )

    rt = toks // tp

    def tp_copy(step):
        to = lax.rem(my_tp + step, tp)
        return copy(
            bc.at[:, pl.ds(pl.multiple_of(to * rt, rt), rt)], rtp.at[step - 1],
            n_tp + step - 1, {"tp": to},
        )

    barrier = pltpu.get_barrier_semaphore()

    def greet(to):
        pl.semaphore_signal(barrier, inc=1, device_id=to, device_id_type=MESH)

    expected = tp - 1
    if two:
        greet({"ctx": core_mate})
        expected = expected + 1
    if four:
        greet({"ctx": side_mate})
        expected = expected + 1
    for step in range(1, tp):
        greet({"tp": lax.rem(my_tp + step, tp)})

    @pl.when(place > 0)
    def _():
        greet({"ctx": me - group})

    @pl.when(place < groups - 1)
    def _():
        greet({"ctx": me + group})

    inner = jnp.where(place > 0, 1, 0) + jnp.where(place < groups - 1, 1, 0)

    row_i = lax.broadcasted_iota(jnp.int32, (toks, toks), 0)
    col_i = lax.broadcasted_iota(jnp.int32, (toks, toks), 1)
    low_left = lax.broadcasted_iota(jnp.int32, (toks, LANES), 1) < HALF
    left_mid = lax.broadcasted_iota(jnp.int32, (mid, LANES), 1) < HALF
    lane = lax.broadcasted_iota(jnp.int32, (toks, LANES), 1)

    def cols(q):
        return pl.ds(pl.multiple_of(q * LANES, LANES), LANES)

    codes = code_ref[...]
    code_high = lax.shift_right_logical(codes, 8).astype(F32)
    code_low = (codes & 255).astype(F32)
    upto = (col_i <= row_i).astype(BF16)
    run_high = dot(upto, code_high.astype(BF16), NT)
    run_low = dot(upto, code_low.astype(BF16), NT)
    total = run_high * 256.0 + run_low
    within_col = total * (-CODE_UNIT)

    head_row = lax.broadcasted_iota(jnp.int32, (heads, toks), 0)
    del head_row
    rows_acc[...] = jnp.zeros_like(rows_acc)
    rows_acc[0:heads, :] = (
        dot(code_high.astype(BF16), (row_i <= col_i).astype(BF16)) * 256.0
        + dot(code_low.astype(BF16), (row_i <= col_i).astype(BF16))
    ) * (-CODE_UNIT)
    for q in range(pairs):
        wl[:, q * LANES:(q + 1) * LANES] = jnp.where(
            low_left, within_col[:, 2 * q:2 * q + 1], within_col[:, 2 * q + 1:2 * q + 2]
        )
    dec[...] = jnp.zeros_like(dec)
    for q in range(pairs):
        dec[q:q + 1, :] = jnp.exp(wl[toks - 1:toks, q * LANES:(q + 1) * LANES])

    b_high, b_low = parts(b_ref[...])
    c_high, c_low = parts(c_ref[...])
    bwide[...] = jnp.concatenate([b_high, b_low], axis=1)
    cwide[...] = jnp.concatenate([c_high, c_low], axis=1)
    b_tall = jnp.transpose(jnp.concatenate([b_high.astype(F32), b_low.astype(F32)], axis=1)).astype(BF16)
    c_tall = jnp.transpose(jnp.concatenate([c_high.astype(F32), c_low.astype(F32)], axis=1)).astype(BF16)

    def weighted(q):
        w = wl[:, cols(q)]
        tail = jnp.exp(wl[pl.ds(toks - 1, 1), cols(q)] - w)
        return tail, jnp.exp(w)

    def local_state(q):
        tail, head = weighted(q)
        for d, (tall, value) in enumerate(
            ((b_tall, tail * x_ref[:, cols(q)]), (c_tall, head * g_ref[:, cols(q)]))
        ):
            high, low = parts(value)
            out = dot(tall, jnp.concatenate([high, low], axis=1))
            out = out[:LANES] + out[LANES:]
            loc[d, q] = out[:, :LANES] + out[:, LANES:]

    def loop(count, body):
        lax.fori_loop(0, count, lambda k, _: (body(k), 0)[1], 0)

    if two:
        loop(hp, lambda k: local_state((1 - core) * hp + k))
    else:
        loop(hp, local_state)
    pl.semaphore_wait(barrier, expected + inner)
    if two:
        dec0_copy().start()
        up0(0).start()
        up0(1).start()
        loop(hp, lambda k: local_state(half0 + k))

    score[...] = (
        dot(b_high, c_high, NT) + dot(b_high, c_low, NT) + dot(b_low, c_high, NT)
    )
    dscore[...] = jnp.zeros_like(dscore)
    col_acc[...] = jnp.zeros_like(col_acc)
    colq_acc[...] = jnp.zeros_like(colq_acc)
    bc[...] = jnp.zeros_like(bc)
    causal = row_i <= col_i

    def intra(q):
        x = x_ref[:, cols(q)]
        g = g_ref[:, cols(q)]
        w = wl[:, cols(q)]
        xh = x.astype(BF16).astype(F32)
        xl = x - xh
        gh = g.astype(BF16).astype(F32)
        gl = g - gh
        xl_s, gh_s, gl_s, w_s = swap(xl), swap(gh), swap(gl), swap(w)
        xh_b, gh_b = xh.astype(BF16), gh.astype(BF16)
        zero = jnp.zeros_like(g)
        results = []
        for n in range(2):
            if n == 0:
                pick = lambda a, b: jnp.where(low_left, a, b)
            else:
                pick = lambda a, b: jnp.where(low_left, b, a)
            left = jnp.concatenate([pick(xh, xl_s).astype(BF16), xh_b], axis=1)
            right = jnp.concatenate([pick(gh, gh_s).astype(BF16), pick(gl, zero).astype(BF16)], axis=1)
            value = pick(gh, gl_s).astype(BF16)
            w_here = pick(w, w_s)
            row = rows_acc[pl.ds(2 * q + n, 1), :]
            out = []
            colsum = []
            rowsum = []
            for r in range(2):
                here = slice(r * mid, (r + 1) * mid)
                after = slice(r * mid, toks)
                width = toks - r * mid
                wh = w_here[here]
                wide = jnp.concatenate([wh] * (width // LANES), axis=1)
                gap = jnp.where(causal[here, after], row[:, after] - wide, -1e30)
                decay = jnp.exp(gap)
                dm = dot(left[here], right[after], NT)
                scaled = dm * decay
                sc = score[here, after]
                dscore[here, after] += scaled
                z = scaled * sc
                colsum.append(jnp.sum(z, axis=0, keepdims=True))
                rowsum.append(jnp.sum(z, axis=1, keepdims=True))
                mh, ml = parts(decay * sc)
                main = dot(mh, value[after])
                out.append(main + swap(main) + dot(ml, gh_b[after]))
            results.append(jnp.concatenate(out, axis=0))
            rows_acc[pl.ds(2 * q + n, 1), :] = jnp.concatenate(
                [colsum[0][:, :mid], colsum[0][:, mid:] + colsum[1]], axis=1
            )
            col_acc[...] -= jnp.where(lane == 2 * q + n, jnp.concatenate(rowsum, axis=0), 0.0)
        dx_ref[:, cols(q)] = jnp.where(low_left, results[0], results[1])

    ticks = groups - 1 + qp
    early = pairs // 5
    loop(early, intra)

    if two:
        dec0_copy().wait()
        up0(0).wait()
        up0(1).wait()
        dec1[...] = dec[...] * rdec0[...]

        def join(d, k):
            own_first = core == d
            q = half0 + k
            one = jnp.ones((1, LANES), F32)
            mine, other = dec[pl.ds(q, 1), :], rdec0[pl.ds(q, 1), :]
            agg[d, k] = (
                jnp.where(own_first, other, one) * loc[d, q]
                + jnp.where(own_first, one, mine) * rbuf0[d, k]
            )

        if four:
            dec1_copy().start()

            def out_up(k):
                for d in range(2):
                    join(d, (1 - side) * qp + k)
                    up1(d, k).start()

            loop(qp, out_up)

        def keep(k):
            for d in range(2):
                join(d, mine0 + k)

        loop(qp, keep)
    else:
        dec1[...] = dec[...]

        def keep(k):
            for d in range(2):
                agg[d, k] = loc[d, k]

        loop(qp, keep)
    if four:
        dec1_copy().wait()

    def finish_core(d, k):
        q = half0 + k
        z = zp[d, k]
        if not two:
            ent[d, q] = z
            return
        own_first = core == d
        first_dec = jnp.where(own_first, dec[pl.ds(q, 1), :], rdec0[pl.ds(q, 1), :])
        first = jnp.where(own_first, loc[d, q], rbuf0[d, k])
        later = first_dec * z + first
        ent[d, q] = jnp.where(own_first, z, later)
        snd0[d, k] = jnp.where(own_first, later, z)
        down0(d, k).start()

    def carry(d, k):
        q = half0 + mine0 + k
        has_before = place > 0 if d == 0 else place < groups - 1
        has_after = place < groups - 1 if d == 0 else place > 0
        own = agg[d, mine0 + k]
        mine = dec1[pl.ds(q, 1), :]
        if four:
            up1(d, k).wait_recv()
            other = rdec1[pl.ds(q, 1), :]
            got = rbuf1[d, k]
            own_first = side == d
            one = jnp.ones((1, LANES), F32)
            full = jnp.where(own_first, other, one) * own + jnp.where(own_first, one, mine) * got
            full_dec = mine * other
        else:
            full, full_dec = own, mine

        @pl.when(has_before)
        def _():
            chain(d, k).wait_recv()

        @pl.when(jnp.logical_not(has_before))
        def _():
            zin[d, k] = jnp.zeros((LANES, LANES), F32)

        z = zin[d, k]

        @pl.when(has_after)
        def _():
            zout[d, k] = full_dec * z + full
            chain(d, k).start()

        if four:
            first_dec = jnp.where(own_first, mine, other)
            later = first_dec * z + jnp.where(own_first, own, got)
            snd1[d, k] = jnp.where(own_first, later, z)
            down1(d, k).start()
            zp[d, mine0 + k] = jnp.where(own_first, z, later)
        else:
            zp[d, mine0 + k] = z
        finish_core(d, mine0 + k)

    per = -(-(pairs - early) // ticks)

    def tick(t):
        for d in range(2):
            k = t - place if d == 0 else t - (groups - 1 - place)

            @pl.when(jnp.logical_and(k >= 0, k < qp))
            def _():
                carry(d, k)

        for j in range(per):
            q = early + t * per + j

            @pl.when(q < pairs)
            def _():
                intra(q)

    loop(ticks, tick)

    ones_row = lax.broadcasted_iota(jnp.int32, (toks, LANES), 0) == toks - 1

    def inter(q):
        tail, head = weighted(q)
        x = x_ref[:, cols(q)]
        sh, sl = parts(ent[0, q])
        gh, gl = parts(ent[1, q])
        eg = head * g_ref[:, cols(q)]
        tx = tail * x
        s_wide = jnp.concatenate([sh, sl], axis=1)
        g_wide = jnp.concatenate([gh, gl], axis=1)
        y = dot(cwide[...], jnp.concatenate([s_wide, s_wide], axis=0))
        y = y[:, :LANES] + y[:, LANES:]
        dxi = dot(bwide[...], jnp.concatenate([g_wide, g_wide], axis=0))
        dxi = tail * (dxi[:, :LANES] + dxi[:, LANES:])
        dx_ref[:, cols(q)] += dxi
        s_tall = jnp.concatenate([sh, sl], axis=0)
        g_tall = jnp.concatenate([gh, gl], axis=0)
        dc = dot(jnp.concatenate(parts(eg), axis=1), jnp.concatenate([s_tall, s_tall], axis=1), NT)
        bc[1] += dc[:, :LANES] + dc[:, LANES:]
        db = dot(jnp.concatenate(parts(tx), axis=1), jnp.concatenate([g_tall, g_tall], axis=1), NT)
        bc[0] += db[:, :LANES] + db[:, LANES:]
        across = jnp.sum(ent[0, q] * ent[1, q], axis=0, keepdims=True) * dec[pl.ds(q, 1), :]
        read = eg * y
        read = read + jnp.where(ones_row, across, 0.0)
        wrote = x * dxi
        for n in range(2):
            mask = low_left if n == 0 else jnp.logical_not(low_left)
            here = lane == 2 * q + n
            col_acc[...] += jnp.where(here, jnp.sum(jnp.where(mask, read, 0.0), axis=1, keepdims=True), 0.0)
            colq_acc[...] += jnp.where(here, jnp.sum(jnp.where(mask, wrote, 0.0), axis=1, keepdims=True), 0.0)

    if four:
        def side_in(k):
            inter(half0 + mine0 + k)
            for d in range(2):
                down1(d, k).wait_recv()
                finish_core(d, (1 - side) * qp + k)

        loop(qp, side_in)
        loop(qp, lambda k: inter(half0 + (1 - side) * qp + k))
    else:
        loop(hp, lambda k: inter(half0 + k))

    if two:
        def core_in(k):
            for d in range(2):
                down0(d, k).wait_recv()
            inter((1 - core) * hp + k)

        if four:
            loop(qp, lambda k: core_in(mine0 + k))
            loop(qp, lambda k: core_in((1 - side) * qp + k))
        else:
            loop(hp, core_in)

    dsh, dsl = parts(dscore[...])
    bc[0] += dot(dsh, c_high) + dot(dsh, c_low) + dot(dsl, c_high)
    bc[1] += dot(dsh, b_high, TN) + dot(dsh, b_low, TN) + dot(dsl, b_high, TN)
    for step in range(1, tp):
        tp_copy(step).start()

    later = (row_i >= col_i).astype(BF16)
    earlier = (row_i < col_i).astype(BF16)
    grad = exact_dot(col_acc[...], later, TN) + exact_dot(colq_acc[...], earlier, TN)
    da_ref[...] = grad[:heads] + exact_dot(rows_acc[0:heads, :], later, NN)

    own_rows = pl.ds(pl.multiple_of(my_tp * rt, rt), rt)
    db_sum = bc[0, own_rows]
    dc_sum = bc[1, own_rows]
    for step in range(1, tp):
        tp_copy(step).wait_recv()
        db_sum = db_sum + rtp[step - 1, 0]
        dc_sum = dc_sum + rtp[step - 1, 1]
    db_ref[...] = db_sum
    dc_ref[...] = dc_sum

    for step in range(1, tp):
        tp_copy(step).wait_send()

    def left(k):
        for d in range(2):
            has_after = place < groups - 1 if d == 0 else place > 0
            if four:
                up1(d, k).wait_send()
                down1(d, k).wait_send()

            @pl.when(has_after)
            def _():
                chain(d, k).wait_send()

    loop(qp, left)
    if two:
        def left_core(k):
            for d in range(2):
                down0(d, k).wait_send()

        loop(hp, left_core)


def per_device(ctx, tp, x, b, c, codes, g):
    heads, toks = codes.shape
    pairs = x.shape[1] // LANES
    hp = pairs // 2 if pairs % 2 == 0 else pairs
    qp = pairs // 4 if pairs % 4 == 0 else hp
    pad = -(-pairs // 8) * 8
    state = (LANES, LANES)
    copies = 4 + 6 * qp + 2 * hp + tp - 1
    vmem = pl.BlockSpec(memory_space=pltpu.VMEM)
    shape = jax.ShapeDtypeStruct
    return pl.pallas_call(
        functools.partial(kernel, ctx, tp),
        out_shape=(
            shape(x.shape, F32), shape((toks // tp, LANES), F32),
            shape((toks // tp, LANES), F32), shape(codes.shape, F32),
        ),
        in_specs=[vmem] * 5,
        out_specs=(vmem,) * 4,
        scratch_shapes=[
            pltpu.VMEM(x.shape, F32),
            pltpu.VMEM((2, pairs) + state, F32),
            pltpu.VMEM((pad, LANES), F32),
            pltpu.VMEM((pad, LANES), F32),
            pltpu.VMEM((pad, LANES), F32),
            pltpu.VMEM((pad, LANES), F32),
            pltpu.VMEM((2, hp) + state, F32),
            pltpu.VMEM((2, hp) + state, F32),
            pltpu.VMEM((2, qp) + state, F32),
            pltpu.VMEM((2, qp) + state, F32),
            pltpu.VMEM((2, qp) + state, F32),
            pltpu.VMEM((2, hp) + state, F32),
            pltpu.VMEM((2, qp) + state, F32),
            pltpu.VMEM((2, hp) + state, F32),
            pltpu.VMEM((2, pairs) + state, F32),
            pltpu.VMEM((toks, toks), F32),
            pltpu.VMEM((toks, toks), F32),
            pltpu.VMEM((-(-heads // 8) * 8, toks), F32),
            pltpu.VMEM((toks, LANES), F32),
            pltpu.VMEM((toks, LANES), F32),
            pltpu.VMEM((2, toks, LANES), F32),
            pltpu.VMEM((max(tp - 1, 1), 2, toks // tp, LANES), F32),
            pltpu.VMEM((toks, 2 * LANES), BF16),
            pltpu.VMEM((toks, 2 * LANES), BF16),
            pltpu.SemaphoreType.DMA((copies,)),
            pltpu.SemaphoreType.DMA((copies,)),
        ],
        compiler_params=pltpu.CompilerParams(
            collective_id=0, has_side_effects=True, vmem_limit_bytes=50 * 1024 * 1024
        ),
    )(x, b, c, codes, g)


def solution(mesh):
    placed = (P("ctx", "tp"), P("ctx", None), P("ctx", None), P("tp", "ctx"), P("ctx", "tp"))
    return jax.shard_map(
        functools.partial(per_device, mesh.shape["ctx"], mesh.shape["tp"]),
        mesh=mesh,
        in_specs=placed,
        out_specs=(P("ctx", "tp"), P(("ctx", "tp"), None), P(("ctx", "tp"), None), P("tp", "ctx")),
        check_vma=False,
    )
```

time: 341 us -> 67.9 us (0.20)
  waiting for transfers between devices: 187 us -> 0 us
  Pallas kernels: 0 us -> 61.1 us
  matrix products: 56.2 us -> 0 us
  blocking collectives: 35.9 us -> 0 us
  other arithmetic: 31.5 us -> 0 us
  between operations: 14.8 us -> 0.65 us
  local copies, waits for them, and re-layouts: 12.9 us -> 5.95 us
    all_gather x2 -> x0, waiting for transfers between devices: 150 us -> none  [carried_in(): gathered = jax.tree.map(lambda a: lax.all_gather(a, axis), part)]
    pallas_call x0 -> x1, Pallas kernels: none -> 61.1 us  [per_device(): pl.pallas_call(functools.partial(kernel, ctx, tp), out_shape=(shape(x.sha...]
    dot_general x11 -> x0, matrix products: 56.2 us -> none  [the longest x2 29.1 us: ssd_forward(): jnp.einsum('hkts,hksp->hktp', decay_matrix * scores[None], values, precis...]
    reduce_scatter x2 -> x0, waiting for transfers between devices: 36.8 us -> none  [the longest x1 36.8 us: per_device(): lax.psum_scatter(reader_grad.reshape(row_count, state_width), 'tp', scatt...]
    unnamed x1 -> x0, blocking collectives: 35.9 us -> none
    add x15 -> x0, other arithmetic: 23.7 us -> none  [combine_states(): later[0][:, None, None] * earlier[1] + later[1]]
    unnamed x35 -> x10, local copies, waits for them, and re-layouts: 11.5 us -> 5.95 us
    another operation x5 -> x0, other arithmetic: 3.82 us -> none
  transfers between devices with their start and end apart: 4 -> 0, of which waited for: 3 -> 0; matrix products, arithmetic and copies ran while one was open for 15% -> 0% of each run, Pallas kernels for 0% -> 0%
where the time goes in v1:
time: 67.9 us; the launch traced here: 67.7 us
  Pallas kernels  61.1 us (90%)
  local copies, waits for them, and re-layouts  5.95 us (9%)
    pallas_call x1, Pallas kernels, per_device(): pl.pallas_call(functools.partial(kernel, ctx, tp), out_shape=(shape(x.sha...  61.1 us
    unnamed x10, local copies, waits for them, and re-layouts  5.95 us

profile of v1, /device:TPU:0, one launch (start us, length us, event | category | flops | bytes accessed | tf_op | source)
XLA Modules:
  0.0 67.7 jit_solution(16830919240469435853)
XLA Ops:
  0.6 0.0 copy-start
  0.6 0.9 %copy-done = f32[256,128]{1,0:T(8,128)S(1)} copy-done((f32[256,128]{1,0:T(8,128)S(1)}, f32[256,128]{1,0:T(8,128)}, u32[]{:S(2)}) %copy-start) | copy-done | bytes 131096
  1.5 0.0 copy-start.1
  1.5 0.9 %copy-done.1 = f32[256,128]{1,0:T(8,128)S(1)} copy-done((f32[256,128]{1,0:T(8,128)S(1)}, f32[256,128]{1,0:T(8,128)}, u32[]{:S(2)}) %copy-start.1) | copy-done | bytes 131096
  2.4 0.0 copy-start.2
  2.4 0.8 %copy-done.2 = s32[40,256]{1,0:T(8,128)S(1)} copy-done((s32[40,256]{1,0:T(8,128)S(1)}, s32[40,256]{1,0:T(8,128)}, u32[]{:S(2)}) %copy-start.2) | copy-done | bytes 40984
  3.2 61.1 %shard_map.84 = (f32[256,2560]{1,0:T(8,128)S(1)}, f32[128,128]{1,0:T(8,128)S(1)}, f32[128,128]{1,0:T(8,128)S(1)}, f32[40,256]{1,0:T(8,128)S(1)}) custom-call(f32[256,2560]{1,0:T(8,128)} %x_ref.1, f32[256,128]{1,0:T(8,128)S(1)} %copy-done, f32[256,128]{1,0:T(8,128)S(1)} %copy-done.1, s32[40,256]{1,0:T(8,128)S(1)} %copy-done.2, f32[256,2560]{1,0:T(8,128)} %g_ref.1), custom_call_target="tpu_custom_call" | custom-call | tf_op jit(solution)/shard_map/pallas_call | solution.py:504
  64.4 1.5 %copy.13 = f32[256,2560]{1,0:T(8,128)} copy(f32[256,2560]{1,0:T(8,128)S(1)} %get-tuple-element.8) | data formatting | bytes 5242880
  65.9 0.6 copy.14
  66.5 0.6 copy.15
  67.1 0.6 copy.16
Async XLA Ops:
  0.6 0.9 %copy-start = (f32[256,128]{1,0:T(8,128)S(1)}, f32[256,128]{1,0:T(8,128)}, u32[]{:S(2)}) copy-start(f32[256,128]{1,0:T(8,128)} %b_ref.1) | copy-start | bytes 393220
  1.5 0.9 %copy-start.1 = (f32[256,128]{1,0:T(8,128)S(1)}, f32[256,128]{1,0:T(8,128)}, u32[]{:S(2)}) copy-start(f32[256,128]{1,0:T(8,128)} %c_ref.1) | copy-start | bytes 393220
  2.4 0.8 %copy-start.2 = (s32[40,256]{1,0:T(8,128)S(1)}, s32[40,256]{1,0:T(8,128)}, u32[]{:S(2)}) copy-start(s32[40,256]{1,0:T(8,128)} %code_ref.1) | copy-start | bytes 122884

commit v2 on v1

--- a/solution.py
+++ b/solution.py
@@ -40,11 +40,11 @@
 
 
 def kernel(
-    ctx, tp, x_ref, b_ref, c_ref, code_ref, g_ref,
+    ctx, tp, x_hbm, b_hbm, c_hbm, code_hbm, g_hbm,
     dx_ref, db_ref, dc_ref, da_ref,
     wl, loc, dec, rdec0, dec1, rdec1, rbuf0, agg, rbuf1, zin, zout, zp, snd1, snd0, ent,
     score, dscore, rows_acc, col_acc, colq_acc, bc, rtp,
-    cwide, bwide, send, recv,
+    cwide, bwide, x_ref, g_ref, b_ref, c_ref, code_ref, send, recv, fetched,
 ):
     heads, toks = code_ref.shape
     pairs = x_ref.shape[1] // LANES
@@ -66,8 +66,34 @@
     half0 = core * hp if two else 0
     mine0 = side * qp if four else 0
 
-    n_dec1 = 3
-    n_up = 4
+    if four:
+        starts = [h * hp + s * qp for s in (1 - side, side) for h in (1 - core, core)]
+    elif two:
+        starts = [(1 - core) * hp, core * hp]
+    else:
+        starts = [0]
+
+    def fetch(number):
+        if number < 3:
+            src, dst = ((code_hbm, code_ref), (b_hbm, b_ref), (c_hbm, c_ref))[number]
+            return pltpu.make_async_copy(src, dst, fetched.at[number])
+        part, which = (number - 3) // 2, (number - 3) % 2
+        src, dst = ((x_hbm, x_ref), (g_hbm, g_ref))[which]
+        span = pl.ds(pl.multiple_of(starts[part] * LANES, LANES), qp * LANES)
+        return pltpu.make_async_copy(src.at[:, span], dst.at[:, span], fetched.at[number])
+
+    def arrived(*which):
+        for part in which:
+            fetch(3 + 2 * part).wait()
+            fetch(4 + 2 * part).wait()
+
+    for number in range(3 + 2 * len(starts)):
+        fetch(number).start()
+
+    n_dec0 = 0
+    n_dec1 = 1
+    n_first = 2
+    n_up = n_first + 2 * hp
     n_chain = n_up + 2 * qp
     n_down = n_chain + 2 * qp
     n_last = n_down + 2 * qp
@@ -79,19 +105,21 @@
             device_id=to, device_id_type=MESH,
         )
 
-    def up0(d):
-        there = (1 - core) * hp
-        return copy(loc.at[d, pl.ds(there, hp)], rbuf0.at[d], d, {"ctx": core_mate})
+    def up0(d, k):
+        return copy(
+            loc.at[d, (1 - core) * hp + k], rbuf0.at[d, k], n_first + d * hp + k,
+            {"ctx": core_mate},
+        )
 
     def dec0_copy():
-        return copy(dec, rdec0, 2, {"ctx": core_mate})
+        return copy(dec, rdec0, n_dec0, {"ctx": core_mate})
 
     def dec1_copy():
         return copy(dec1, rdec1, n_dec1, {"ctx": side_mate})
 
     def up1(d, k):
         return copy(
-            agg.at[d, (1 - side) * qp + k], rbuf1.at[d, k], n_up + d * qp + k, {"ctx": side_mate}
+            agg.at[d, k], rbuf1.at[d, k], n_up + d * qp + k, {"ctx": side_mate}
         )
 
     def chain(d, k):
@@ -151,6 +179,7 @@
     def cols(q):
         return pl.ds(pl.multiple_of(q * LANES, LANES), LANES)
 
+    fetch(0).wait()
     codes = code_ref[...]
     code_high = lax.shift_right_logical(codes, 8).astype(F32)
     code_low = (codes & 255).astype(F32)
@@ -160,8 +189,6 @@
     total = run_high * 256.0 + run_low
     within_col = total * (-CODE_UNIT)
 
-    head_row = lax.broadcasted_iota(jnp.int32, (heads, toks), 0)
-    del head_row
     rows_acc[...] = jnp.zeros_like(rows_acc)
     rows_acc[0:heads, :] = (
         dot(code_high.astype(BF16), (row_i <= col_i).astype(BF16)) * 256.0
@@ -175,6 +202,8 @@
     for q in range(pairs):
         dec[q:q + 1, :] = jnp.exp(wl[toks - 1:toks, q * LANES:(q + 1) * LANES])
 
+    fetch(1).wait()
+    fetch(2).wait()
     b_high, b_low = parts(b_ref[...])
     c_high, c_low = parts(c_ref[...])
     bwide[...] = jnp.concatenate([b_high, b_low], axis=1)
@@ -200,16 +229,54 @@
     def loop(count, body):
         lax.fori_loop(0, count, lambda k, _: (body(k), 0)[1], 0)
 
-    if two:
-        loop(hp, lambda k: local_state((1 - core) * hp + k))
-    else:
-        loop(hp, local_state)
     pl.semaphore_wait(barrier, expected + inner)
+
+    def make(k):
+        local_state((1 - core) * hp + k)
+        for d in range(2):
+            up0(d, k).start()
+        local_state(half0 + k)
+
+    def join(d, k):
+        own_first = core == d
+        q = half0 + k
+        one = jnp.ones((1, LANES), F32)
+        mine, other = dec[pl.ds(q, 1), :], rdec0[pl.ds(q, 1), :]
+        up0(d, k).wait_recv()
+        return (
+            jnp.where(own_first, other, one) * loc[d, q]
+            + jnp.where(own_first, one, mine) * rbuf0[d, k]
+        )
+
+    def pass_up(k):
+        for d in range(2):
+            agg[d, k] = join(d, (1 - side) * qp + k)
+            up1(d, k).start()
+
     if two:
         dec0_copy().start()
-        up0(0).start()
-        up0(1).start()
-        loop(hp, lambda k: local_state(half0 + k))
+        arrived(0, 1)
+        other0 = (1 - side) * qp if four else 0
+        make(other0)
+        dec0_copy().wait()
+        dec1[...] = dec[...] * rdec0[...]
+        if four:
+            dec1_copy().start()
+
+            def step_up(k):
+                make(other0 + k + 1)
+                pass_up(k)
+
+            loop(qp - 1, step_up)
+            pass_up(qp - 1)
+            arrived(2, 3)
+            loop(qp, lambda k: make(mine0 + k))
+        else:
+            loop(qp - 1, lambda k: make(k + 1))
+    else:
+        arrived(0)
+        loop(pairs, local_state)
+        dec1[...] = dec[...]
 
     score[...] = (
         dot(b_high, c_high, NT) + dot(b_high, c_low, NT) + dot(b_low, c_high, NT)
@@ -218,6 +285,7 @@
     col_acc[...] = jnp.zeros_like(col_acc)
     colq_acc[...] = jnp.zeros_like(colq_acc)
     bc[...] = jnp.zeros_like(bc)
+    dx_ref[...] = jnp.zeros_like(dx_ref)
     causal = row_i <= col_i
 
     def intra(q):
@@ -268,51 +336,10 @@
                 [colsum[0][:, :mid], colsum[0][:, mid:] + colsum[1]], axis=1
             )
             col_acc[...] -= jnp.where(lane == 2 * q + n, jnp.concatenate(rowsum, axis=0), 0.0)
-        dx_ref[:, cols(q)] = jnp.where(low_left, results[0], results[1])
-
-    ticks = groups - 1 + qp
-    early = pairs // 5
+        dx_ref[:, cols(q)] += jnp.where(low_left, results[0], results[1])
+
+    early = pairs // 4
     loop(early, intra)
-
-    if two:
-        dec0_copy().wait()
-        up0(0).wait()
-        up0(1).wait()
-        dec1[...] = dec[...] * rdec0[...]
-
-        def join(d, k):
-            own_first = core == d
-            q = half0 + k
-            one = jnp.ones((1, LANES), F32)
-            mine, other = dec[pl.ds(q, 1), :], rdec0[pl.ds(q, 1), :]
-            agg[d, k] = (
-                jnp.where(own_first, other, one) * loc[d, q]
-                + jnp.where(own_first, one, mine) * rbuf0[d, k]
-            )
-
-        if four:
-            dec1_copy().start()
-
-            def out_up(k):
-                for d in range(2):
-                    join(d, (1 - side) * qp + k)
-                    up1(d, k).start()
-
-            loop(qp, out_up)
-
-        def keep(k):
-            for d in range(2):
-                join(d, mine0 + k)
-
-        loop(qp, keep)
-    else:
-        dec1[...] = dec[...]
-
-        def keep(k):
-            for d in range(2):
-                agg[d, k] = loc[d, k]
-
-        loop(qp, keep)
     if four:
         dec1_copy().wait()
 
@@ -334,7 +361,7 @@
         q = half0 + mine0 + k
         has_before = place > 0 if d == 0 else place < groups - 1
         has_after = place < groups - 1 if d == 0 else place > 0
-        own = agg[d, mine0 + k]
+        own = join(d, mine0 + k) if two else loc[d, k]
         mine = dec1[pl.ds(q, 1), :]
         if four:
             up1(d, k).wait_recv()
@@ -371,25 +398,6 @@
         else:
             zp[d, mine0 + k] = z
         finish_core(d, mine0 + k)
-
-    per = -(-(pairs - early) // ticks)
-
-    def tick(t):
-        for d in range(2):
-            k = t - place if d == 0 else t - (groups - 1 - place)
-
-            @pl.when(jnp.logical_and(k >= 0, k < qp))
-            def _():
-                carry(d, k)
-
-        for j in range(per):
-            q = early + t * per + j
-
-            @pl.when(q < pairs)
-            def _():
-                intra(q)
-
-    loop(ticks, tick)
 
     ones_row = lax.broadcasted_iota(jnp.int32, (toks, LANES), 0) == toks - 1
 
@@ -423,29 +431,49 @@
             col_acc[...] += jnp.where(here, jnp.sum(jnp.where(mask, read, 0.0), axis=1, keepdims=True), 0.0)
             colq_acc[...] += jnp.where(here, jnp.sum(jnp.where(mask, wrote, 0.0), axis=1, keepdims=True), 0.0)
 
-    if four:
+    both = jnp.maximum(place, groups - 1 - place)
+    lag = 2 if four else 1 if two else 0
+    intra_ticks = groups + 1
+    per = -(-(pairs - early) // intra_ticks)
+
+    def tick(t):
+        def when_in(k, body):
+            @pl.when(jnp.logical_and(k >= 0, k < qp))
+            def _():
+                body(k)
+
+        for d in range(2):
+            when_in(t - (place if d == 0 else groups - 1 - place), functools.partial(carry, d))
+        now = t - both
+
         def side_in(k):
-            inter(half0 + mine0 + k)
             for d in range(2):
                 down1(d, k).wait_recv()
                 finish_core(d, (1 - side) * qp + k)
 
-        loop(qp, side_in)
-        loop(qp, lambda k: inter(half0 + (1 - side) * qp + k))
-    else:
-        loop(hp, lambda k: inter(half0 + k))
-
-    if two:
         def core_in(k):
             for d in range(2):
                 down0(d, k).wait_recv()
             inter((1 - core) * hp + k)
 
         if four:
-            loop(qp, lambda k: core_in(mine0 + k))
-            loop(qp, lambda k: core_in((1 - side) * qp + k))
-        else:
-            loop(hp, core_in)
+            when_in(now - 1, side_in)
+        for j in range(per):
+            q = early + t * per + j
+
+            @pl.when(q < pairs)
+            def _():
+                intra(q)
+
+        when_in(now, lambda k: inter(half0 + mine0 + k))
+        if four:
+            when_in(now - 1, lambda k: inter(half0 + (1 - side) * qp + k))
+        if two:
+            when_in(now - 1, lambda k: core_in(mine0 + k))
+        if four:
+            when_in(now - 2, lambda k: core_in((1 - side) * qp + k))
+
+    loop(groups - 1 + qp + lag, tick)
 
     dsh, dsl = parts(dscore[...])
     bc[0] += dot(dsh, c_high) + dot(dsh, c_low) + dot(dsl, c_high)
@@ -486,9 +514,22 @@
     if two:
         def left_core(k):
             for d in range(2):
+                up0(d, k).wait_send()
                 down0(d, k).wait_send()
 
         loop(hp, left_core)
+
+
+def store(*refs):
+    done = refs[-1]
+    half = (len(refs) - 1) // 2
+    copies = [
+        pltpu.make_async_copy(refs[n], refs[half + n], done.at[n]) for n in range(half)
+    ]
+    for one in copies:
+        one.start()
+    for one in copies:
+        one.wait()
 
 
 def per_device(ctx, tp, x, b, c, codes, g):
@@ -498,16 +539,16 @@
     qp = pairs // 4 if pairs % 4 == 0 else hp
     pad = -(-pairs // 8) * 8
     state = (LANES, LANES)
-    copies = 4 + 6 * qp + 2 * hp + tp - 1
+    copies = 2 + 6 * qp + 4 * hp + tp - 1
     vmem = pl.BlockSpec(memory_space=pltpu.VMEM)
     shape = jax.ShapeDtypeStruct
-    return pl.pallas_call(
+    outs = pl.pallas_call(
         functools.partial(kernel, ctx, tp),
         out_shape=(
             shape(x.shape, F32), shape((toks // tp, LANES), F32),
             shape((toks // tp, LANES), F32), shape(codes.shape, F32),
         ),
-        in_specs=[vmem] * 5,
+        in_specs=[pl.BlockSpec(memory_space=pltpu.HBM)] * 5,
         out_specs=(vmem,) * 4,
         scratch_shapes=[
             pltpu.VMEM(x.shape, F32),
@@ -517,7 +558,7 @@
             pltpu.VMEM((pad, LANES), F32),
             pltpu.VMEM((pad, LANES), F32),
             pltpu.VMEM((2, hp) + state, F32),
-            pltpu.VMEM((2, hp) + state, F32),
+            pltpu.VMEM((2, qp) + state, F32),
             pltpu.VMEM((2, qp) + state, F32),
             pltpu.VMEM((2, qp) + state, F32),
             pltpu.VMEM((2, qp) + state, F32),
@@ -534,13 +575,27 @@
             pltpu.VMEM((max(tp - 1, 1), 2, toks // tp, LANES), F32),
             pltpu.VMEM((toks, 2 * LANES), BF16),
             pltpu.VMEM((toks, 2 * LANES), BF16),
+            pltpu.VMEM(x.shape, F32),
+            pltpu.VMEM(x.shape, F32),
+            pltpu.VMEM(b.shape, F32),
+            pltpu.VMEM(c.shape, F32),
+            pltpu.VMEM(codes.shape, jnp.int32),
             pltpu.SemaphoreType.DMA((copies,)),
             pltpu.SemaphoreType.DMA((copies,)),
+            pltpu.SemaphoreType.DMA((11,)),
         ],
         compiler_params=pltpu.CompilerParams(
             collective_id=0, has_side_effects=True, vmem_limit_bytes=50 * 1024 * 1024
         ),
     )(x, b, c, codes, g)
+    return pl.pallas_call(
+        store,
+        out_shape=tuple(shape(one.shape, F32) for one in outs),
+        in_specs=[vmem] * 4,
+        out_specs=(pl.BlockSpec(memory_space=pltpu.HBM),) * 4,
+        scratch_shapes=[pltpu.SemaphoreType.DMA((4,))],
+        compiler_params=pltpu.CompilerParams(vmem_limit_bytes=8 * 1024 * 1024),
+    )(*outs)
 
 
 def solution(mesh):

time: 67.9 us -> 60.7 us (0.89)
  Pallas kernels: 61.1 us -> 57.3 us
  local copies, waits for them, and re-layouts: 5.95 us -> 2.58 us
    pallas_call x1, Pallas kernels: 61.1 us -> 55.7 us  [per_device(): pl.pallas_call(functools.partial(kernel, ctx, tp), out_shape=(shape(x.sha...]
    unnamed x10 -> x6, local copies, waits for them, and re-layouts: 5.95 us -> 2.58 us
    pallas_call x0 -> x1, Pallas kernels: none -> 1.56 us  [per_device(): pl.pallas_call(store, out_shape=tuple((shape(one.shape, F32) for one in o...]
where the time goes in v2:
time: 60.7 us; the launch traced here: 60.5 us
  Pallas kernels  57.3 us (94%)
  local copies, waits for them, and re-layouts  2.58 us (4%)
  between operations  0.65 us (1%)
    pallas_call x1, Pallas kernels, per_device(): pl.pallas_call(functools.partial(kernel, ctx, tp), out_shape=(shape(x.sha...  55.7 us
    unnamed x6, local copies, waits for them, and re-layouts  2.58 us
    pallas_call x1, Pallas kernels, per_device(): pl.pallas_call(store, out_shape=tuple((shape(one.shape, F32) for one in o...  1.56 us

profile of v2, /device:TPU:0, one launch (start us, length us, event | category | flops | bytes accessed | tf_op | source)
XLA Modules:
  0.0 60.5 jit_solution(13951776787579994827)
XLA Ops:
  0.6 0.0 copy-start
  0.6 0.9 %copy-done = f32[256,128]{1,0:T(8,128)S(1)} copy-done((f32[256,128]{1,0:T(8,128)S(1)}, f32[256,128]{1,0:T(8,128)}, u32[]{:S(2)}) %copy-start) | copy-done | bytes 131096
  1.5 0.0 copy-start.1
  1.5 0.9 %copy-done.1 = f32[256,128]{1,0:T(8,128)S(1)} copy-done((f32[256,128]{1,0:T(8,128)S(1)}, f32[256,128]{1,0:T(8,128)}, u32[]{:S(2)}) %copy-start.1) | copy-done | bytes 131096
  2.4 0.0 copy-start.2
  2.4 0.8 %copy-done.2 = s32[40,256]{1,0:T(8,128)S(1)} copy-done((s32[40,256]{1,0:T(8,128)S(1)}, s32[40,256]{1,0:T(8,128)}, u32[]{:S(2)}) %copy-start.2) | copy-done | bytes 40984
  3.2 55.7 %shard_map.84 = (f32[256,2560]{1,0:T(8,128)S(1)}, f32[128,128]{1,0:T(8,128)S(1)}, f32[128,128]{1,0:T(8,128)S(1)}, f32[40,256]{1,0:T(8,128)S(1)}) custom-call(f32[256,2560]{1,0:T(8,128)} %x_hbm.1, f32[256,128]{1,0:T(8,128)S(1)} %copy-done, f32[256,128]{1,0:T(8,128)S(1)} %copy-done.1, s32[40,256]{1,0:T(8,128)S(1)} %copy-done.2, f32[256,2560]{1,0:T(8,128)} %g_hbm.1), custom_call_target="tpu_custom_call" | custom-call | tf_op jit(solution)/shard_map/pallas_call | solution.py:545
  59.0 1.6 %shard_map.85 = (f32[256,2560]{1,0:T(8,128)}, f32[128,128]{1,0:T(8,128)}, f32[128,128]{1,0:T(8,128)}, f32[40,256]{1,0:T(8,128)}) custom-call(f32[256,2560]{1,0:T(8,128)S(1)} %get-tuple-element.8.refs_0_, f32[128,128]{1,0:T(8,128)S(1)} %get-tuple-element.9.refs_1_, f32[128,128]{1,0:T(8,128)S(1)} %get-tuple-element.10.refs_2_, ...), custom_call_target="tpu_custom_call" | custom-call | tf_op jit(solution)/shard_map/pallas_call | solution.py:591
Async XLA Ops:
  0.6 0.9 %copy-start = (f32[256,128]{1,0:T(8,128)S(1)}, f32[256,128]{1,0:T(8,128)}, u32[]{:S(2)}) copy-start(f32[256,128]{1,0:T(8,128)} %b_hbm.1) | copy-start | bytes 393220
  1.5 0.9 %copy-start.1 = (f32[256,128]{1,0:T(8,128)S(1)}, f32[256,128]{1,0:T(8,128)}, u32[]{:S(2)}) copy-start(f32[256,128]{1,0:T(8,128)} %c_hbm.1) | copy-start | bytes 393220
  2.4 0.8 %copy-start.2 = (s32[40,256]{1,0:T(8,128)S(1)}, s32[40,256]{1,0:T(8,128)}, u32[]{:S(2)}) copy-start(s32[40,256]{1,0:T(8,128)} %code_hbm.1) | copy-start | bytes 122884

commit v3 on v2

--- a/solution.py
+++ b/solution.py
@@ -40,13 +40,13 @@
 
 
 def kernel(
-    ctx, tp, x_hbm, b_hbm, c_hbm, code_hbm, g_hbm,
+    ctx, tp, x_hbm, g_hbm, small_ref,
     dx_ref, db_ref, dc_ref, da_ref,
     wl, loc, dec, rdec0, dec1, rdec1, rbuf0, agg, rbuf1, zin, zout, zp, snd1, snd0, ent,
-    score, dscore, rows_acc, col_acc, colq_acc, bc, rtp,
-    cwide, bwide, x_ref, g_ref, b_ref, c_ref, code_ref, send, recv, fetched,
+    score, dscore, w_rows, rows_acc, rowsq_acc, bc, rtp,
+    cwide, bwide, wides, x_ref, g_ref, send, recv, fetched,
 ):
-    heads, toks = code_ref.shape
+    heads, toks = da_ref.shape
     pairs = x_ref.shape[1] // LANES
     two = pairs % 2 == 0
     four = pairs % 4 == 0
@@ -74,20 +74,17 @@
         starts = [0]
 
     def fetch(number):
-        if number < 3:
-            src, dst = ((code_hbm, code_ref), (b_hbm, b_ref), (c_hbm, c_ref))[number]
-            return pltpu.make_async_copy(src, dst, fetched.at[number])
-        part, which = (number - 3) // 2, (number - 3) % 2
+        part, which = number // 2, number % 2
         src, dst = ((x_hbm, x_ref), (g_hbm, g_ref))[which]
         span = pl.ds(pl.multiple_of(starts[part] * LANES, LANES), qp * LANES)
         return pltpu.make_async_copy(src.at[:, span], dst.at[:, span], fetched.at[number])
 
     def arrived(*which):
         for part in which:
-            fetch(3 + 2 * part).wait()
-            fetch(4 + 2 * part).wait()
-
-    for number in range(3 + 2 * len(starts)):
+            fetch(2 * part).wait()
+            fetch(2 * part + 1).wait()
+
+    for number in range(2 * len(starts)):
         fetch(number).start()
 
     n_dec0 = 0
@@ -173,24 +170,23 @@
     row_i = lax.broadcasted_iota(jnp.int32, (toks, toks), 0)
     col_i = lax.broadcasted_iota(jnp.int32, (toks, toks), 1)
     low_left = lax.broadcasted_iota(jnp.int32, (toks, LANES), 1) < HALF
-    left_mid = lax.broadcasted_iota(jnp.int32, (mid, LANES), 1) < HALF
-    lane = lax.broadcasted_iota(jnp.int32, (toks, LANES), 1)
 
     def cols(q):
         return pl.ds(pl.multiple_of(q * LANES, LANES), LANES)
 
-    fetch(0).wait()
-    codes = code_ref[...]
-    code_high = lax.shift_right_logical(codes, 8).astype(F32)
-    code_low = (codes & 255).astype(F32)
+    codes = small_ref[toks:toks + heads, 0:toks]
+    code_high = jnp.floor(codes * (1.0 / 256.0))
+    code_low = codes - code_high * 256.0
     upto = (col_i <= row_i).astype(BF16)
     run_high = dot(upto, code_high.astype(BF16), NT)
     run_low = dot(upto, code_low.astype(BF16), NT)
     total = run_high * 256.0 + run_low
     within_col = total * (-CODE_UNIT)
 
+    w_rows[...] = jnp.zeros_like(w_rows)
     rows_acc[...] = jnp.zeros_like(rows_acc)
-    rows_acc[0:heads, :] = (
+    rowsq_acc[...] = jnp.zeros_like(rowsq_acc)
+    w_rows[0:heads, :] = (
         dot(code_high.astype(BF16), (row_i <= col_i).astype(BF16)) * 256.0
         + dot(code_low.astype(BF16), (row_i <= col_i).astype(BF16))
     ) * (-CODE_UNIT)
@@ -202,10 +198,8 @@
     for q in range(pairs):
         dec[q:q + 1, :] = jnp.exp(wl[toks - 1:toks, q * LANES:(q + 1) * LANES])
 
-    fetch(1).wait()
-    fetch(2).wait()
-    b_high, b_low = parts(b_ref[...])
-    c_high, c_low = parts(c_ref[...])
+    b_high, b_low = parts(small_ref[0:toks, :LANES])
+    c_high, c_low = parts(small_ref[0:toks, LANES:])
     bwide[...] = jnp.concatenate([b_high, b_low], axis=1)
     cwide[...] = jnp.concatenate([c_high, c_low], axis=1)
     b_tall = jnp.transpose(jnp.concatenate([b_high.astype(F32), b_low.astype(F32)], axis=1)).astype(BF16)
@@ -222,7 +216,9 @@
             ((b_tall, tail * x_ref[:, cols(q)]), (c_tall, head * g_ref[:, cols(q)]))
         ):
             high, low = parts(value)
-            out = dot(tall, jnp.concatenate([high, low], axis=1))
+            wide = jnp.concatenate([high, low], axis=1)
+            wides[d, q] = wide
+            out = dot(tall, wide)
             out = out[:LANES] + out[LANES:]
             loc[d, q] = out[:, :LANES] + out[:, LANES:]
 
@@ -233,9 +229,9 @@
 
     def make(k):
         local_state((1 - core) * hp + k)
+        local_state(half0 + k)
         for d in range(2):
             up0(d, k).start()
-        local_state(half0 + k)
 
     def join(d, k):
         own_first = core == d
@@ -282,64 +278,83 @@
         dot(b_high, c_high, NT) + dot(b_high, c_low, NT) + dot(b_low, c_high, NT)
     )
     dscore[...] = jnp.zeros_like(dscore)
-    col_acc[...] = jnp.zeros_like(col_acc)
-    colq_acc[...] = jnp.zeros_like(colq_acc)
     bc[...] = jnp.zeros_like(bc)
     dx_ref[...] = jnp.zeros_like(dx_ref)
     causal = row_i <= col_i
 
-    def intra(q):
-        x = x_ref[:, cols(q)]
-        g = g_ref[:, cols(q)]
-        w = wl[:, cols(q)]
-        xh = x.astype(BF16).astype(F32)
-        xl = x - xh
-        gh = g.astype(BF16).astype(F32)
-        gl = g - gh
-        xl_s, gh_s, gl_s, w_s = swap(xl), swap(gh), swap(gl), swap(w)
-        xh_b, gh_b = xh.astype(BF16), gh.astype(BF16)
-        zero = jnp.zeros_like(g)
-        results = []
-        for n in range(2):
-            if n == 0:
-                pick = lambda a, b: jnp.where(low_left, a, b)
-            else:
-                pick = lambda a, b: jnp.where(low_left, b, a)
-            left = jnp.concatenate([pick(xh, xl_s).astype(BF16), xh_b], axis=1)
-            right = jnp.concatenate([pick(gh, gh_s).astype(BF16), pick(gl, zero).astype(BF16)], axis=1)
-            value = pick(gh, gl_s).astype(BF16)
-            w_here = pick(w, w_s)
-            row = rows_acc[pl.ds(2 * q + n, 1), :]
-            out = []
-            colsum = []
-            rowsum = []
-            for r in range(2):
-                here = slice(r * mid, (r + 1) * mid)
-                after = slice(r * mid, toks)
-                width = toks - r * mid
-                wh = w_here[here]
-                wide = jnp.concatenate([wh] * (width // LANES), axis=1)
-                gap = jnp.where(causal[here, after], row[:, after] - wide, -1e30)
-                decay = jnp.exp(gap)
-                dm = dot(left[here], right[after], NT)
-                scaled = dm * decay
-                sc = score[here, after]
-                dscore[here, after] += scaled
-                z = scaled * sc
-                colsum.append(jnp.sum(z, axis=0, keepdims=True))
-                rowsum.append(jnp.sum(z, axis=1, keepdims=True))
-                mh, ml = parts(decay * sc)
-                main = dot(mh, value[after])
-                out.append(main + swap(main) + dot(ml, gh_b[after]))
-            results.append(jnp.concatenate(out, axis=0))
-            rows_acc[pl.ds(2 * q + n, 1), :] = jnp.concatenate(
-                [colsum[0][:, :mid], colsum[0][:, mid:] + colsum[1]], axis=1
-            )
-            col_acc[...] -= jnp.where(lane == 2 * q + n, jnp.concatenate(rowsum, axis=0), 0.0)
-        dx_ref[:, cols(q)] += jnp.where(low_left, results[0], results[1])
+    def head_rows(a):
+        turned = jnp.transpose(a)
+        return [jnp.sum(turned[n * HALF:(n + 1) * HALF], axis=0, keepdims=True) for n in range(2)]
+
+    def intra(*pair_list):
+        pair_rows = [[w_rows[pl.ds(2 * q + n, 1), :] for n in range(2)] for q in pair_list]
+        finished = []
+        for q, w_row in zip(pair_list, pair_rows):
+            x = x_ref[:, cols(q)]
+            g = g_ref[:, cols(q)]
+            w = wl[:, cols(q)]
+            xh = x.astype(BF16).astype(F32)
+            xl = x - xh
+            gh = g.astype(BF16).astype(F32)
+            gl = g - gh
+            xl_s, gh_s, gl_s, w_s = swap(xl), swap(gh), swap(gl), swap(w)
+            xh_b, gh_b = xh.astype(BF16), gh.astype(BF16)
+            zero = jnp.zeros_like(g)
+            results, folded, colsums = [], [], []
+            for n in range(2):
+                if n == 0:
+                    pick = lambda a, b: jnp.where(low_left, a, b)
+                else:
+                    pick = lambda a, b: jnp.where(low_left, b, a)
+                left = jnp.concatenate([pick(xh, xl_s).astype(BF16), xh_b], axis=1)
+                right = jnp.concatenate(
+                    [pick(gh, gh_s).astype(BF16), pick(gl, zero).astype(BF16)], axis=1
+                )
+                value = pick(gh, gl_s).astype(BF16)
+                w_here = pick(w, w_s)
+                dm = dot(left, right, NT)
+                high, low, fold, colsum = [], [], [], []
+                for r in range(2):
+                    here = slice(r * mid, (r + 1) * mid)
+                    after = slice(r * mid, toks)
+                    width = toks - r * mid
+                    wide = jnp.concatenate([w_here[here]] * (width // LANES), axis=1)
+                    gap = jnp.where(causal[here, after], w_row[n][:, after] - wide, -1e30)
+                    decay = jnp.exp(gap)
+                    scaled = dm[here, after] * decay
+                    sc = score[here, after]
+                    dscore[here, after] += scaled
+                    z = scaled * sc
+                    colsum.append(jnp.sum(z, axis=0, keepdims=True))
+                    fold.append(sum(z[:, i * LANES:(i + 1) * LANES] for i in range(width // LANES)))
+                    mh, ml = parts(decay * sc)
+                    if r:
+                        nothing = jnp.zeros((mid, mid), BF16)
+                        mh = jnp.concatenate([nothing, mh], axis=1)
+                        ml = jnp.concatenate([nothing, ml], axis=1)
+                    high.append(mh)
+                    low.append(ml)
+                main = dot(jnp.concatenate(high, axis=0), value)
+                results.append(main + swap(main) + dot(jnp.concatenate(low, axis=0), gh_b))
+                fold = jnp.concatenate(fold, axis=0)
+                folded.append(fold + swap(fold))
+                colsums.append(
+                    jnp.concatenate([colsum[0][:, :mid], colsum[0][:, mid:] + colsum[1]], axis=1)
+                )
+            rowsums = head_rows(jnp.where(low_left, folded[0], folded[1]))
+            finished.append((
+                jnp.where(low_left, results[0], results[1]),
+                [colsums[n] - rowsums[n] for n in range(2)],
+            ))
+        for q, (dx, rows) in zip(pair_list, finished):
+            dx_ref[:, cols(q)] += dx
+            for n in range(2):
+                rows_acc[pl.ds(2 * q + n, 1), :] += rows[n]
 
     early = pairs // 4
-    loop(early, intra)
+    loop(early // 2, lambda k: intra(2 * k, 2 * k + 1))
+    if early % 2:
+        intra(early - 1)
     if four:
         dec1_copy().wait()
 
@@ -401,35 +416,36 @@
 
     ones_row = lax.broadcasted_iota(jnp.int32, (toks, LANES), 0) == toks - 1
 
-    def inter(q):
-        tail, head = weighted(q)
-        x = x_ref[:, cols(q)]
-        sh, sl = parts(ent[0, q])
-        gh, gl = parts(ent[1, q])
-        eg = head * g_ref[:, cols(q)]
-        tx = tail * x
-        s_wide = jnp.concatenate([sh, sl], axis=1)
-        g_wide = jnp.concatenate([gh, gl], axis=1)
-        y = dot(cwide[...], jnp.concatenate([s_wide, s_wide], axis=0))
-        y = y[:, :LANES] + y[:, LANES:]
-        dxi = dot(bwide[...], jnp.concatenate([g_wide, g_wide], axis=0))
-        dxi = tail * (dxi[:, :LANES] + dxi[:, LANES:])
-        dx_ref[:, cols(q)] += dxi
-        s_tall = jnp.concatenate([sh, sl], axis=0)
-        g_tall = jnp.concatenate([gh, gl], axis=0)
-        dc = dot(jnp.concatenate(parts(eg), axis=1), jnp.concatenate([s_tall, s_tall], axis=1), NT)
-        bc[1] += dc[:, :LANES] + dc[:, LANES:]
-        db = dot(jnp.concatenate(parts(tx), axis=1), jnp.concatenate([g_tall, g_tall], axis=1), NT)
-        bc[0] += db[:, :LANES] + db[:, LANES:]
-        across = jnp.sum(ent[0, q] * ent[1, q], axis=0, keepdims=True) * dec[pl.ds(q, 1), :]
-        read = eg * y
-        read = read + jnp.where(ones_row, across, 0.0)
-        wrote = x * dxi
-        for n in range(2):
-            mask = low_left if n == 0 else jnp.logical_not(low_left)
-            here = lane == 2 * q + n
-            col_acc[...] += jnp.where(here, jnp.sum(jnp.where(mask, read, 0.0), axis=1, keepdims=True), 0.0)
-            colq_acc[...] += jnp.where(here, jnp.sum(jnp.where(mask, wrote, 0.0), axis=1, keepdims=True), 0.0)
+    def inter(*pair_list):
+        db_sum, dc_sum = 0.0, 0.0
+        finished = []
+        for q in pair_list:
+            tail = jnp.exp(wl[pl.ds(toks - 1, 1), cols(q)] - wl[:, cols(q)])
+            sh, sl = parts(ent[0, q])
+            gh, gl = parts(ent[1, q])
+            tx, eg = wides[0, q], wides[1, q]
+            s_wide = jnp.concatenate([sh, sl], axis=1)
+            g_wide = jnp.concatenate([gh, gl], axis=1)
+            y = dot(cwide[...], jnp.concatenate([s_wide, s_wide], axis=0))
+            y = y[:, :LANES] + y[:, LANES:]
+            dxi = dot(bwide[...], jnp.concatenate([g_wide, g_wide], axis=0))
+            dxi = dxi[:, :LANES] + dxi[:, LANES:]
+            s_tall = jnp.concatenate([sh, sl], axis=0)
+            g_tall = jnp.concatenate([gh, gl], axis=0)
+            dc_sum += dot(eg, jnp.concatenate([s_tall, s_tall], axis=1), NT)
+            db_sum += dot(tx, jnp.concatenate([g_tall, g_tall], axis=1), NT)
+            across = jnp.sum(ent[0, q] * ent[1, q], axis=0, keepdims=True) * dec[pl.ds(q, 1), :]
+            read = (eg[:, :LANES].astype(F32) + eg[:, LANES:].astype(F32)) * y
+            read = read + jnp.where(ones_row, across, 0.0)
+            wrote = (tx[:, :LANES].astype(F32) + tx[:, LANES:].astype(F32)) * dxi
+            finished.append((tail * dxi, head_rows(read), head_rows(wrote)))
+        bc[0] += db_sum[:, :LANES] + db_sum[:, LANES:]
+        bc[1] += dc_sum[:, :LANES] + dc_sum[:, LANES:]
+        for q, (dx, rows, rowsq) in zip(pair_list, finished):
+            dx_ref[:, cols(q)] += dx
+            for n in range(2):
+                rows_acc[pl.ds(2 * q + n, 1), :] += rows[n]
+                rowsq_acc[pl.ds(2 * q + n, 1), :] = rowsq[n]
 
     both = jnp.maximum(place, groups - 1 - place)
     lag = 2 if four else 1 if two else 0
@@ -451,27 +467,42 @@
                 down1(d, k).wait_recv()
                 finish_core(d, (1 - side) * qp + k)
 
-        def core_in(k):
+        def core_wait(k):
             for d in range(2):
                 down0(d, k).wait_recv()
-            inter((1 - core) * hp + k)
+
+        def first_three(k):
+            core_wait(mine0 + k)
+            inter(half0 + mine0 + k, half0 + (1 - side) * qp + k, (1 - core) * hp + mine0 + k)
+
+        def last_one(k):
+            core_wait((1 - side) * qp + k)
+            inter((1 - core) * hp + (1 - side) * qp + k)
+
+        def first_two(k):
+            core_wait(k)
+            inter(half0 + k, (1 - core) * hp + k)
 
         if four:
             when_in(now - 1, side_in)
-        for j in range(per):
-            q = early + t * per + j
-
-            @pl.when(q < pairs)
+        q0 = early + t * per
+        if (pairs - early) % per == 0:
+            @pl.when(q0 < pairs)
             def _():
-                intra(q)
-
-        when_in(now, lambda k: inter(half0 + mine0 + k))
+                intra(*[q0 + j for j in range(per)])
+        else:
+            for j in range(per):
+                @pl.when(q0 + j < pairs)
+                def _():
+                    intra(q0 + j)
+
         if four:
-            when_in(now - 1, lambda k: inter(half0 + (1 - side) * qp + k))
-        if two:
-            when_in(now - 1, lambda k: core_in(mine0 + k))
-        if four:
-            when_in(now - 2, lambda k: core_in((1 - side) * qp + k))
+            when_in(now - 1, first_three)
+            when_in(now - 2, last_one)
+        elif two:
+            when_in(now - 1, first_two)
+        else:
+            when_in(now, inter)
 
     loop(groups - 1 + qp + lag, tick)
 
@@ -483,8 +514,9 @@
 
     later = (row_i >= col_i).astype(BF16)
     earlier = (row_i < col_i).astype(BF16)
-    grad = exact_dot(col_acc[...], later, TN) + exact_dot(colq_acc[...], earlier, TN)
-    da_ref[...] = grad[:heads] + exact_dot(rows_acc[0:heads, :], later, NN)
+    da_ref[...] = exact_dot(rows_acc[0:heads, :], later, NN) + exact_dot(
+        rowsq_acc[0:heads, :], earlier, NN
+    )
 
     own_rows = pl.ds(pl.multiple_of(my_tp * rt, rt), rt)
     db_sum = bc[0, own_rows]
@@ -542,13 +574,17 @@
     copies = 2 + 6 * qp + 4 * hp + tp - 1
     vmem = pl.BlockSpec(memory_space=pltpu.VMEM)
     shape = jax.ShapeDtypeStruct
+    small = (
+        jnp.pad(b, ((0, heads), (0, LANES))) + jnp.pad(c, ((0, heads), (LANES, 0)))
+        + jnp.pad(codes.astype(F32), ((toks, 0), (0, 2 * LANES - toks)))
+    )
     outs = pl.pallas_call(
         functools.partial(kernel, ctx, tp),
         out_shape=(
             shape(x.shape, F32), shape((toks // tp, LANES), F32),
             shape((toks // tp, LANES), F32), shape(codes.shape, F32),
         ),
-        in_specs=[pl.BlockSpec(memory_space=pltpu.HBM)] * 5,
+        in_specs=[pl.BlockSpec(memory_space=pltpu.HBM)] * 2 + [vmem],
         out_specs=(vmem,) * 4,
         scratch_shapes=[
             pltpu.VMEM(x.shape, F32),
@@ -569,25 +605,23 @@
             pltpu.VMEM((toks, toks), F32),
             pltpu.VMEM((toks, toks), F32),
             pltpu.VMEM((-(-heads // 8) * 8, toks), F32),
-            pltpu.VMEM((toks, LANES), F32),
-            pltpu.VMEM((toks, LANES), F32),
+            pltpu.VMEM((-(-heads // 8) * 8, toks), F32),
+            pltpu.VMEM((-(-heads // 8) * 8, toks), F32),
             pltpu.VMEM((2, toks, LANES), F32),
             pltpu.VMEM((max(tp - 1, 1), 2, toks // tp, LANES), F32),
             pltpu.VMEM((toks, 2 * LANES), BF16),
             pltpu.VMEM((toks, 2 * LANES), BF16),
+            pltpu.VMEM((2, pairs, toks, 2 * LANES), BF16),
             pltpu.VMEM(x.shape, F32),
             pltpu.VMEM(x.shape, F32),
-            pltpu.VMEM(b.shape, F32),
-            pltpu.VMEM(c.shape, F32),
-            pltpu.VMEM(codes.shape, jnp.int32),
             pltpu.SemaphoreType.DMA((copies,)),
             pltpu.SemaphoreType.DMA((copies,)),
-            pltpu.SemaphoreType.DMA((11,)),
+            pltpu.SemaphoreType.DMA((8,)),
         ],
         compiler_params=pltpu.CompilerParams(
             collective_id=0, has_side_effects=True, vmem_limit_bytes=50 * 1024 * 1024
         ),
-    )(x, b, c, codes, g)
+    )(x, g, small)
     return pl.pallas_call(
         store,
         out_shape=tuple(shape(one.shape, F32) for one in outs),

time: 60.7 us -> 54.5 us (0.90)
  Pallas kernels: 57.3 us -> 51.9 us
  local copies, waits for them, and re-layouts: 2.58 us -> 0 us
  other arithmetic: 0 us -> 1.77 us
    pallas_call x1, Pallas kernels: 55.7 us -> 50.3 us  [per_device(): pl.pallas_call(functools.partial(kernel, ctx, tp), out_shape=(shape(x.sha...]
    unnamed x6 -> x0, local copies, waits for them, and re-layouts: 2.58 us -> none
    add x0 -> x1, other arithmetic: none -> 0.99 us  [per_device(): jnp.pad(b, ((0, heads), (0, LANES))) + jnp.pad(c, ((0, heads), (LANES, 0)))]
    convert_element_type x0 -> x1, other arithmetic: none -> 0.78 us  [per_device(): codes.astype(F32)]
where the time goes in v3:
time: 54.5 us; the launch traced here: 54.3 us
  Pallas kernels  51.9 us (95%)
  other arithmetic  1.77 us (3%)
  between operations  0.64 us (1%)
    pallas_call x1, Pallas kernels, per_device(): pl.pallas_call(functools.partial(kernel, ctx, tp), out_shape=(shape(x.sha...  50.3 us
    pallas_call x1, Pallas kernels, per_device(): pl.pallas_call(store, out_shape=tuple((shape(one.shape, F32) for one in o...  1.56 us

profile of v3, /device:TPU:0, one launch (start us, length us, event | category | flops | bytes accessed | tf_op | source)
XLA Modules:
  0.0 54.3 jit_solution(12085828149438683520)
XLA Ops:
  0.6 0.8 %convert_element_type.9 = f32[40,256]{1,0:T(8,128)S(1)} convert(s32[40,256]{1,0:T(8,128)} %param.8) | non-fusion elementwise | flops 10240 | bytes 81920 | tf_op jit(solution)/shard_map/convert_element_type | solution.py:579
  1.4 1.0 %pad_add_fusion.small_ref = f32[296,256]{1,0:T(8,128)S(1)} fusion(f32[40,256]{1,0:T(8,128)S(1)} %convert_element_type.9, f32[256,128]{1,0:T(8,128)} %param.7, f32[256,128]{1,0:T(8,128)} %param.6), kind=kLoop, calls=%fused_computation | loop fusion | flops 151552 | bytes 606208 | tf_op jit(solution)/shard_map/add | solution.py:578
  2.4 50.3 %shard_map.84 = (f32[256,2560]{1,0:T(8,128)S(1)}, f32[128,128]{1,0:T(8,128)S(1)}, f32[128,128]{1,0:T(8,128)S(1)}, f32[40,256]{1,0:T(8,128)S(1)}) custom-call(f32[256,2560]{1,0:T(8,128)} %x_hbm.1, f32[256,2560]{1,0:T(8,128)} %g_hbm.1, f32[296,256]{1,0:T(8,128)S(1)} %pad_add_fusion.small_ref), custom_call_target="tpu_custom_call" | custom-call | tf_op jit(solution)/shard_map/pallas_call | solution.py:581
  52.7 1.6 %shard_map.85 = (f32[256,2560]{1,0:T(8,128)}, f32[128,128]{1,0:T(8,128)}, f32[128,128]{1,0:T(8,128)}, f32[40,256]{1,0:T(8,128)}) custom-call(f32[256,2560]{1,0:T(8,128)S(1)} %get-tuple-element.8.refs_0_, f32[128,128]{1,0:T(8,128)S(1)} %get-tuple-element.9.refs_1_, f32[128,128]{1,0:T(8,128)S(1)} %get-tuple-element.10.refs_2_, ...), custom_call_target="tpu_custom_call" | custom-call | tf_op jit(solution)/shard_map/pallas_call | solution.py:625

commit v4 on v3

--- a/solution.py
+++ b/solution.py
@@ -351,10 +351,6 @@
             for n in range(2):
                 rows_acc[pl.ds(2 * q + n, 1), :] += rows[n]
 
-    early = pairs // 4
-    loop(early // 2, lambda k: intra(2 * k, 2 * k + 1))
-    if early % 2:
-        intra(early - 1)
     if four:
         dec1_copy().wait()
 
@@ -416,41 +412,52 @@
 
     ones_row = lax.broadcasted_iota(jnp.int32, (toks, LANES), 0) == toks - 1
 
-    def inter(*pair_list):
+    def inter_bc(*pair_list):
         db_sum, dc_sum = 0.0, 0.0
+        for q in pair_list:
+            s_tall = jnp.concatenate(parts(ent[0, q]), axis=0)
+            g_tall = jnp.concatenate(parts(ent[1, q]), axis=0)
+            dc_sum += dot(wides[1, q], jnp.concatenate([s_tall, s_tall], axis=1), NT)
+            db_sum += dot(wides[0, q], jnp.concatenate([g_tall, g_tall], axis=1), NT)
+        bc[0] += db_sum[:, :LANES] + db_sum[:, LANES:]
+        bc[1] += dc_sum[:, :LANES] + dc_sum[:, LANES:]
+
+    def inter_dx(*pair_list):
         finished = []
         for q in pair_list:
             tail = jnp.exp(wl[pl.ds(toks - 1, 1), cols(q)] - wl[:, cols(q)])
-            sh, sl = parts(ent[0, q])
-            gh, gl = parts(ent[1, q])
             tx, eg = wides[0, q], wides[1, q]
-            s_wide = jnp.concatenate([sh, sl], axis=1)
-            g_wide = jnp.concatenate([gh, gl], axis=1)
+            s_wide = jnp.concatenate(parts(ent[0, q]), axis=1)
+            g_wide = jnp.concatenate(parts(ent[1, q]), axis=1)
             y = dot(cwide[...], jnp.concatenate([s_wide, s_wide], axis=0))
             y = y[:, :LANES] + y[:, LANES:]
             dxi = dot(bwide[...], jnp.concatenate([g_wide, g_wide], axis=0))
             dxi = dxi[:, :LANES] + dxi[:, LANES:]
-            s_tall = jnp.concatenate([sh, sl], axis=0)
-            g_tall = jnp.concatenate([gh, gl], axis=0)
-            dc_sum += dot(eg, jnp.concatenate([s_tall, s_tall], axis=1), NT)
-            db_sum += dot(tx, jnp.concatenate([g_tall, g_tall], axis=1), NT)
             across = jnp.sum(ent[0, q] * ent[1, q], axis=0, keepdims=True) * dec[pl.ds(q, 1), :]
             read = (eg[:, :LANES].astype(F32) + eg[:, LANES:].astype(F32)) * y
             read = read + jnp.where(ones_row, across, 0.0)
             wrote = (tx[:, :LANES].astype(F32) + tx[:, LANES:].astype(F32)) * dxi
             finished.append((tail * dxi, head_rows(read), head_rows(wrote)))
-        bc[0] += db_sum[:, :LANES] + db_sum[:, LANES:]
-        bc[1] += dc_sum[:, :LANES] + dc_sum[:, LANES:]
         for q, (dx, rows, rowsq) in zip(pair_list, finished):
             dx_ref[:, cols(q)] += dx
             for n in range(2):
                 rows_acc[pl.ds(2 * q + n, 1), :] += rows[n]
                 rowsq_acc[pl.ds(2 * q + n, 1), :] = rowsq[n]
 
+    def inter(*pair_list):
+        inter_bc(*pair_list)
+        inter_dx(*pair_list)
+
+    def within_block():
+        dsh, dsl = parts(dscore[...])
+        bc[0] += dot(dsh, c_high) + dot(dsh, c_low) + dot(dsl, c_high)
+        bc[1] += dot(dsh, b_high, TN) + dot(dsh, b_low, TN) + dot(dsl, b_high, TN)
+
     both = jnp.maximum(place, groups - 1 - place)
     lag = 2 if four else 1 if two else 0
     intra_ticks = groups + 1
-    per = -(-(pairs - early) // intra_ticks)
+    per = -(-pairs // intra_ticks)
+    ticks = groups - 1 + qp + lag
 
     def tick(t):
         def when_in(k, body):
@@ -477,7 +484,7 @@
 
         def last_one(k):
             core_wait((1 - side) * qp + k)
-            inter((1 - core) * hp + (1 - side) * qp + k)
+            inter_bc((1 - core) * hp + (1 - side) * qp + k)
 
         def first_two(k):
             core_wait(k)
@@ -485,11 +492,12 @@
 
         if four:
             when_in(now - 1, side_in)
-        q0 = early + t * per
-        if (pairs - early) % per == 0:
+        q0 = t * per
+        if pairs % per == 0:
             @pl.when(q0 < pairs)
             def _():
-                intra(*[q0 + j for j in range(per)])
+                for j in range(0, per, 2):
+                    intra(*[q0 + i for i in range(j, min(j + 2, per))])
         else:
             for j in range(per):
                 @pl.when(q0 + j < pairs)
@@ -504,13 +512,17 @@
         else:
             when_in(now, inter)
 
-    loop(groups - 1 + qp + lag, tick)
-
-    dsh, dsl = parts(dscore[...])
-    bc[0] += dot(dsh, c_high) + dot(dsh, c_low) + dot(dsl, c_high)
-    bc[1] += dot(dsh, b_high, TN) + dot(dsh, b_low, TN) + dot(dsl, b_high, TN)
+        if ticks > intra_ticks:
+            pl.when(t == intra_ticks)(within_block)
+
+    loop(ticks, tick)
+    if ticks <= intra_ticks:
+        within_block()
+
     for step in range(1, tp):
         tp_copy(step).start()
+    if four:
+        inter_dx(*[(1 - core) * hp + (1 - side) * qp + k for k in range(qp)])
 
     later = (row_i >= col_i).astype(BF16)
     earlier = (row_i < col_i).astype(BF16)

time: 54.5 us -> 54.5 us (level)
  no operation moved by 1% of the time
where the time goes in v4:
time: 54.5 us; the launch traced here: 54.3 us
  Pallas kernels  51.9 us (95%)
  other arithmetic  1.77 us (3%)
  between operations  0.64 us (1%)
    pallas_call x1, Pallas kernels, per_device(): pl.pallas_call(functools.partial(kernel, ctx, tp), out_shape=(shape(x.sha...  50.3 us
    pallas_call x1, Pallas kernels, per_device(): pl.pallas_call(store, out_shape=tuple((shape(one.shape, F32) for one in o...  1.56 us

profile of v4, /device:TPU:0, one launch (start us, length us, event | category | flops | bytes accessed | tf_op | source)
XLA Modules:
  0.0 54.3 jit_solution(5728628961783049548)
XLA Ops:
  0.6 0.8 %convert_element_type.9 = f32[40,256]{1,0:T(8,128)S(1)} convert(s32[40,256]{1,0:T(8,128)} %param.8) | non-fusion elementwise | flops 10240 | bytes 81920 | tf_op jit(solution)/shard_map/convert_element_type | solution.py:591
  1.4 1.0 %pad_add_fusion.small_ref = f32[296,256]{1,0:T(8,128)S(1)} fusion(f32[40,256]{1,0:T(8,128)S(1)} %convert_element_type.9, f32[256,128]{1,0:T(8,128)} %param.7, f32[256,128]{1,0:T(8,128)} %param.6), kind=kLoop, calls=%fused_computation | loop fusion | flops 151552 | bytes 606208 | tf_op jit(solution)/shard_map/add | solution.py:590
  2.4 50.3 %shard_map.84 = (f32[256,2560]{1,0:T(8,128)S(1)}, f32[128,128]{1,0:T(8,128)S(1)}, f32[128,128]{1,0:T(8,128)S(1)}, f32[40,256]{1,0:T(8,128)S(1)}) custom-call(f32[256,2560]{1,0:T(8,128)} %x_hbm.1, f32[256,2560]{1,0:T(8,128)} %g_hbm.1, f32[296,256]{1,0:T(8,128)S(1)} %pad_add_fusion.small_ref), custom_call_target="tpu_custom_call" | custom-call | tf_op jit(solution)/shard_map/pallas_call | solution.py:593
  52.7 1.6 %shard_map.85 = (f32[256,2560]{1,0:T(8,128)}, f32[128,128]{1,0:T(8,128)}, f32[128,128]{1,0:T(8,128)}, f32[40,256]{1,0:T(8,128)}) custom-call(f32[256,2560]{1,0:T(8,128)S(1)} %get-tuple-element.8.refs_0_, f32[128,128]{1,0:T(8,128)S(1)} %get-tuple-element.9.refs_1_, f32[128,128]{1,0:T(8,128)S(1)} %get-tuple-element.10.refs_2_, ...), custom_call_target="tpu_custom_call" | custom-call | tf_op jit(solution)/shard_map/pallas_call | solution.py:637

commit v5 on v4

--- a/solution.py
+++ b/solution.py
@@ -40,7 +40,7 @@
 
 
 def kernel(
-    ctx, tp, x_hbm, g_hbm, small_ref,
+    ctx, tp, x_hbm, g_hbm, small_ref, code_ref,
     dx_ref, db_ref, dc_ref, da_ref,
     wl, loc, dec, rdec0, dec1, rdec1, rbuf0, agg, rbuf1, zin, zout, zp, snd1, snd0, ent,
     score, dscore, w_rows, rows_acc, rowsq_acc, bc, rtp,
@@ -174,9 +174,9 @@
     def cols(q):
         return pl.ds(pl.multiple_of(q * LANES, LANES), LANES)
 
-    codes = small_ref[toks:toks + heads, 0:toks]
-    code_high = jnp.floor(codes * (1.0 / 256.0))
-    code_low = codes - code_high * 256.0
+    codes = code_ref[...]
+    code_high = lax.shift_right_logical(codes, 8).astype(F32)
+    code_low = (codes & 255).astype(F32)
     upto = (col_i <= row_i).astype(BF16)
     run_high = dot(upto, code_high.astype(BF16), NT)
     run_low = dot(upto, code_low.astype(BF16), NT)
@@ -297,9 +297,11 @@
             xl = x - xh
             gh = g.astype(BF16).astype(F32)
             gl = g - gh
-            xl_s, gh_s, gl_s, w_s = swap(xl), swap(gh), swap(gl), swap(w)
+            xl_s, gl_s, w_s = swap(xl), swap(gl), swap(w)
+            gh_t = jnp.transpose(gh).astype(BF16)
+            gl_t = jnp.transpose(gl).astype(BF16)
             xh_b, gh_b = xh.astype(BF16), gh.astype(BF16)
-            zero = jnp.zeros_like(g)
+            zero = jnp.zeros((HALF, toks), BF16)
             results, folded, colsums = [], [], []
             for n in range(2):
                 if n == 0:
@@ -307,12 +309,12 @@
                 else:
                     pick = lambda a, b: jnp.where(low_left, b, a)
                 left = jnp.concatenate([pick(xh, xl_s).astype(BF16), xh_b], axis=1)
-                right = jnp.concatenate(
-                    [pick(gh, gh_s).astype(BF16), pick(gl, zero).astype(BF16)], axis=1
-                )
+                own = slice(n * HALF, (n + 1) * HALF)
+                ends = [gl_t[own], zero] if n == 0 else [zero, gl_t[own]]
+                right = jnp.concatenate([gh_t[own], gh_t[own]] + ends, axis=0)
                 value = pick(gh, gl_s).astype(BF16)
                 w_here = pick(w, w_s)
-                dm = dot(left, right, NT)
+                dm = dot(left, right)
                 high, low, fold, colsum = [], [], [], []
                 for r in range(2):
                     here = slice(r * mid, (r + 1) * mid)
@@ -586,17 +588,14 @@
     copies = 2 + 6 * qp + 4 * hp + tp - 1
     vmem = pl.BlockSpec(memory_space=pltpu.VMEM)
     shape = jax.ShapeDtypeStruct
-    small = (
-        jnp.pad(b, ((0, heads), (0, LANES))) + jnp.pad(c, ((0, heads), (LANES, 0)))
-        + jnp.pad(codes.astype(F32), ((toks, 0), (0, 2 * LANES - toks)))
-    )
+    small = jnp.concatenate([b, c], axis=1)
     outs = pl.pallas_call(
         functools.partial(kernel, ctx, tp),
         out_shape=(
             shape(x.shape, F32), shape((toks // tp, LANES), F32),
             shape((toks // tp, LANES), F32), shape(codes.shape, F32),
         ),
-        in_specs=[pl.BlockSpec(memory_space=pltpu.HBM)] * 2 + [vmem],
+        in_specs=[pl.BlockSpec(memory_space=pltpu.HBM)] * 2 + [vmem] * 2,
         out_specs=(vmem,) * 4,
         scratch_shapes=[
             pltpu.VMEM(x.shape, F32),
@@ -633,7 +632,7 @@
         compiler_params=pltpu.CompilerParams(
             collective_id=0, has_side_effects=True, vmem_limit_bytes=50 * 1024 * 1024
         ),
-    )(x, g, small)
+    )(x, g, small, codes)
     return pl.pallas_call(
         store,
         out_shape=tuple(shape(one.shape, F32) for one in outs),

time: 54.5 us -> 54.6 us (level)
  other arithmetic: 1.77 us -> 0.99 us
  local copies, waits for them, and re-layouts: 0 us -> 0.77 us
    add x1 -> x0, other arithmetic: 0.99 us -> none  [per_device(): jnp.pad(b, ((0, heads), (0, LANES))) + jnp.pad(c, ((0, heads), (LANES, 0)))]
    concatenate x0 -> x1, other arithmetic: none -> 0.99 us  [per_device(): small = jnp.concatenate([b, c], axis=1)]
    convert_element_type x1 -> x0, other arithmetic: 0.78 us -> none  [per_device(): codes.astype(F32)]
    unnamed x0 -> x2, local copies, waits for them, and re-layouts: none -> 0.77 us
where the time goes in v5:
time: 54.6 us; the launch traced here: 54.4 us
  Pallas kernels  52 us (95%)
  other arithmetic  0.99 us (2%)
  local copies, waits for them, and re-layouts  0.77 us (1%)
  between operations  0.65 us (1%)
    pallas_call x1, Pallas kernels, per_device(): pl.pallas_call(functools.partial(kernel, ctx, tp), out_shape=(shape(x.sha...  50.5 us
    pallas_call x1, Pallas kernels, per_device(): pl.pallas_call(store, out_shape=tuple((shape(one.shape, F32) for one in o...  1.56 us

profile of v5, /device:TPU:0, one launch (start us, length us, event | category | flops | bytes accessed | tf_op | source)
XLA Modules:
  0.0 54.4 jit_solution(4443518144396682309)
XLA Ops:
  0.6 1.0 %pad_maximum_fusion.small_ref = f32[256,256]{1,0:T(8,128)S(1)} fusion(f32[256,128]{1,0:T(8,128)} %param.7, f32[256,128]{1,0:T(8,128)} %param.6), kind=kLoop, calls=%fused_computation | loop fusion | flops 65536 | bytes 524288 | tf_op jit(solution)/shard_map/concatenate | solution.py:591
  1.6 0.0 copy-start
  1.6 0.8 %copy-done = s32[40,256]{1,0:T(8,128)S(1)} copy-done((s32[40,256]{1,0:T(8,128)S(1)}, s32[40,256]{1,0:T(8,128)}, u32[]{:S(2)}) %copy-start) | copy-done | bytes 40984
  2.4 50.5 %shard_map.84 = (f32[256,2560]{1,0:T(8,128)S(1)}, f32[128,128]{1,0:T(8,128)S(1)}, f32[128,128]{1,0:T(8,128)S(1)}, f32[40,256]{1,0:T(8,128)S(1)}) custom-call(f32[256,2560]{1,0:T(8,128)} %x_hbm.1, f32[256,2560]{1,0:T(8,128)} %g_hbm.1, f32[256,256]{1,0:T(8,128)S(1)} %pad_maximum_fusion.small_ref, s32[40,256]{1,0:T(8,128)S(1)} %copy-done), custom_call_target="tpu_custom_call" | custom-call | tf_op jit(solution)/shard_map/pallas_call | solution.py:592
  52.9 1.6 %shard_map.85 = (f32[256,2560]{1,0:T(8,128)}, f32[128,128]{1,0:T(8,128)}, f32[128,128]{1,0:T(8,128)}, f32[40,256]{1,0:T(8,128)}) custom-call(f32[256,2560]{1,0:T(8,128)S(1)} %get-tuple-element.8.refs_0_, f32[128,128]{1,0:T(8,128)S(1)} %get-tuple-element.9.refs_1_, f32[128,128]{1,0:T(8,128)S(1)} %get-tuple-element.10.refs_2_, ...), custom_call_target="tpu_custom_call" | custom-call | tf_op jit(solution)/shard_map/pallas_call | solution.py:636
Async XLA Ops:
  1.6 0.8 %copy-start = (s32[40,256]{1,0:T(8,128)S(1)}, s32[40,256]{1,0:T(8,128)}, u32[]{:S(2)}) copy-start(s32[40,256]{1,0:T(8,128)} %code_ref.1) | copy-start | bytes 122884
